TPU v7x, 256 devices: a whole 4x4x8 slice. The times are simulated.
256 devices in a mesh: lon: 64 (over z, x, y_hi), lat: 4 (over y_lo, core).
Axes of the slice: x: 4, y: 4 (y_hi: 2, y_lo: 2; y = y_hi * 2 + y_lo), z: 8, core: 2. Of those that a mesh axis runs over, the one named last changes fastest.
Arguments:
- temp: float32 [10, 128, 8192], P(None, 'lat', 'lon'), may hold values from -6 to 6
- salt: float32 [10, 128, 8192], P(None, 'lat', 'lon'), may hold values from -6 to 6
- u_vel: float32 [10, 128, 8192], P(None, 'lat', 'lon'), may hold values from -3 to 3
- v_vel: float32 [10, 128, 8192], P(None, 'lat', 'lon'), may hold values from -3 to 3
- land_sea: int32 [10, 128, 8192], P(None, 'lat', 'lon'), may hold values 0 or 1
- partner: int32 [8192], P('lon'), may hold values from 0 to 8191, as said below
- kappa_h: float32 [10], replicated, may hold values from 0.02 to 0.25
- kappa_v: float32 [9], replicated, may hold values from 0.02 to 0.12
Outputs:
- temp_next: float32 [10, 128, 8192], P(None, 'lat', 'lon')
- salt_next: float32 [10, 128, 8192], P(None, 'lat', 'lon')
Inputs may be any that keep to these rules, and one draw needn't show every extreme that they name: partner[i] = (s - i) mod 8192 for one s; every longitude appears once.
All inputs are finite; a program needn't handle non-finite values. No bound on the sum of `land_sea` on one device may be relied on, other than what follows from the above.
Results may differ from a plain program's by a relative error of at most 0.00005.
Values sent between devices are 32-bit elements; how exact they have to be, the bound alone decides.
A program may use at most 128 MiB of HBM per device.

v0:
```python
import jax
import jax.numpy as jnp
from jax import lax
from jax.sharding import PartitionSpec as P

STEPS = 2


def with_halo(cells, sides, width, closed):
    for axis, dim in sides:
        count = lax.axis_size(axis)
        ends = count if closed else count - 1
        head = lax.slice_in_dim(cells, 0, width, axis=dim)
        tail = lax.slice_in_dim(cells, cells.shape[dim] - width, cells.shape[dim], axis=dim)
        cells = jnp.concatenate(
            [
                lax.ppermute(tail, axis, [(i, (i + 1) % count) for i in range(ends)]),
                cells,
                lax.ppermute(head, axis, [((i + 1) % count, i) for i in range(ends)]),
            ],
            axis=dim,
        )
    return cells


def extend(stack, signs, partner):
    lon_pad = with_halo(stack, (("lon", 3),), 2, True)
    lat_side = with_halo(stack, (("lat", 2),), 2, False)
    rows = stack[:, :, -2:, :][:, :, ::-1, :]
    gathered = lax.all_gather(rows, "lon", axis=3, tiled=True)
    picked = jnp.take(gathered, partner, axis=3)
    picked = picked * signs[:, None, None, None]
    height = stack.shape[2]
    on_top = lax.axis_index("lat") == lax.axis_size("lat") - 1
    upper = jnp.where(on_top, picked, lat_side[:, :, height + 2 :, :])
    lat_pad = jnp.concatenate([lat_side[:, :, : height + 2, :], upper], axis=2)
    return (lon_pad, lat_pad)


def advance(tracer, tr_x, tr_y, vel_x, vel_y, mask_x, mask_y, ocean, kappa_h, kappa_v):
    width = tracer.shape[-1]
    height = tracer.shape[-2]
    diffuse = kappa_h[:, None, None]
    west2, west1, east1, east2 = (
        tr_x[..., 0 : width + 1],
        tr_x[..., 1 : width + 2],
        tr_x[..., 2 : width + 3],
        tr_x[..., 3 : width + 4],
    )
    face_x = (7.0 * (west1 + east1) - (west2 + east2)) / 12.0
    speed_x = 0.5 * (vel_x[..., 1 : width + 2] + vel_x[..., 2 : width + 3])
    open_x = mask_x[..., 1 : width + 2] * mask_x[..., 2 : width + 3]
    flux_x = open_x * (speed_x * face_x - diffuse * (east1 - west1))
    south2, south1, north1, north2 = (
        tr_y[..., 0 : height + 1, :],
        tr_y[..., 1 : height + 2, :],
        tr_y[..., 2 : height + 3, :],
        tr_y[..., 3 : height + 4, :],
    )
    face_y = (7.0 * (south1 + north1) - (south2 + north2)) / 12.0
    speed_y = 0.5 * (vel_y[..., 1 : height + 2, :] + vel_y[..., 2 : height + 3, :])
    open_y = mask_y[..., 1 : height + 2, :] * mask_y[..., 2 : height + 3, :]
    flux_y = open_y * (speed_y * face_y - diffuse * (north1 - south1))
    open_z = ocean[1:] * ocean[:-1]
    flux_z = kappa_v[:, None, None] * open_z * (tracer[:, 1:] - tracer[:, :-1])
    edge = jnp.zeros_like(flux_z[:, :1])
    flux_z = jnp.concatenate([edge, flux_z, edge], axis=1)
    tendency = (
        -(flux_x[..., 1:] - flux_x[..., :-1])
        - (flux_y[..., 1:, :] - flux_y[..., :-1, :])
        + flux_z[:, 1:]
        - flux_z[:, :-1]
    )
    return tracer + ocean * tendency


def local(temp, salt, u_vel, v_vel, land_sea, partner, kappa_h, kappa_v):
    ocean = land_sea.astype(jnp.float32)
    static = jnp.stack([u_vel, v_vel, ocean])
    tracer = jnp.stack([temp, salt])
    tracer_signs = jnp.array([1.0, 1.0], jnp.float32)
    static_x, static_y = extend(static, jnp.array([-1.0, -1.0, 1.0], jnp.float32), partner)
    first = 0
    for step in range(first, STEPS):
        tr_x, tr_y = extend(tracer, tracer_signs, partner)
        tracer = advance(
            tracer,
            tr_x,
            tr_y,
            static_x[0],
            static_y[1],
            static_x[2],
            static_y[2],
            ocean,
            kappa_h,
            kappa_v,
        )
    return (tracer[0], tracer[1])


def solution(mesh):
    in_specs = (
        P(None, "lat", "lon"),
        P(None, "lat", "lon"),
        P(None, "lat", "lon"),
        P(None, "lat", "lon"),
        P(None, "lat", "lon"),
        P("lon"),
        P(),
        P(),
    )
    out_specs = (P(None, "lat", "lon"), P(None, "lat", "lon"))
    return jax.shard_map(local, mesh=mesh, in_specs=in_specs, out_specs=out_specs, check_vma=False)
```

profile of v0, /device:TPU:2, one launch (start us, length us, event | category | flops | bytes accessed | tf_op | source)
XLA Modules:
  0.0 375.0 jit_solution(16049565935112309417)
XLA Ops:
  11.4 2.3 collective-permute-start.4
  13.7 3.8 %collective-permute-start.6 = (f32[2,10,2,128]{3,2,1,0:T(2,128)S(1)}, f32[2,10,2,128]{3,2,1,0:T(2,128)}, u32[]{:S(2)}, u32[]{:S(2)}) collective-permute-start(f32[2,10,2,128]{3,2,1,0:T(2,128)S(1)} %get-tuple-element.29), channel_id=1, source_target_pairs={{0,1},{1,2},{2,3},{4,5},{5,6},{6,7},{8,9},{9,10},{10,11},{12,13},{... | collective-permute-start | bytes 61448 | tf_op jit(solution)/shard_map/ppermute | solution.py:17
  17.8 1.4 collective-permute-start.5
  19.2 1.3 fusion.18
  20.5 3.0 collective-permute-start.2
  23.5 1.5 collective-permute-start.3
  25.0 1.0 pad_maximum_fusion.4
  28.8 1.9 fusion.36
  30.9 7.6 %collective-permute-done.2 = f32[2,10,32,2]{3,2,1,0:T(8,128)S(1)} collective-permute-done((f32[2,10,32,2]{3,2,1,0:T(8,128)S(1)}, f32[2,10,32,2]{3,2,1,0:T(8,128)S(1)}, u32[]{:S(2)}, u32[]{:S(2)}) %collective-permute-start.2) | collective-permute-done | bytes 5152 | tf_op jit(solution)/shard_map/ppermute | solution.py:17
  38.5 4.0 %collective-permute-start = (f32[3,10,32,2]{3,2,1,0:T(8,128)S(1)}, f32[3,10,32,2]{3,2,1,0:T(8,128)S(1)}, u32[]{:S(2)}, u32[]{:S(2)}) collective-permute-start(f32[3,10,32,2]{3,2,1,0:T(8,128)S(1)} %get-tuple-element.13), channel_id=1, source_target_pairs={{0,4},{4,8},{8,12},{12,16},{16,20},{20,24},{24,28},{28,32},{32,36}... | collective-permute-start | bytes 23048 | tf_op jit(solution)/shard_map/ppermute | solution.py:17
  42.9 1.4 maximum_maximum_fusion
  44.3 21.2 %collective-permute-done = f32[3,10,32,2]{3,2,1,0:T(8,128)S(1)} collective-permute-done((f32[3,10,32,2]{3,2,1,0:T(8,128)S(1)}, f32[3,10,32,2]{3,2,1,0:T(8,128)S(1)}, u32[]{:S(2)}, u32[]{:S(2)}) %collective-permute-start) | collective-permute-done | bytes 7712 | tf_op jit(solution)/shard_map/ppermute | solution.py:17
  65.5 1.3 collective-permute-start.7
  66.8 1.2 maximum_bitcast_fusion
  68.5 1.1 fusion.8
  69.6 43.2 %all-gather.6.cloned.1.call-done = f32[2,10,2,8192]{3,2,1,0:T(2,128)} async-done(((f32[2,10,2,128]{3,2,1,0:T(2,128)}), f32[2,10,2,8192]{3,2,1,0:T(2,128)}) %all-gather.6.cloned.1.call-update) | async-done | bytes 1310736 | tf_op jit(solution)/shard_map/all_gather | solution.py:30
  112.7 17.9 %copy.95 = f32[2,10,2,8192]{1,2,3,0:T(2,128)} copy(f32[2,10,2,8192]{3,2,1,0:T(2,128)} %all-gather.6.cloned.1.call-done) | data formatting | bytes 2621440 | tf_op jit(solution)/shard_map/all_gather | solution.py:30
  130.6 6.8 %gather_fusion.1 = f32[128,2,10,2]{2,3,1,0:T(2,128)S(1)} fusion(f32[2,10,2,8192]{1,2,3,0:T(2,128)} %copy.95, s32[1024]{0:T(1024)S(1)} %pad_clamp_fusion), kind=kCustom, calls=%fused_computation.clone | custom fusion | bytes 41472 | tf_op jit(solution)/shard_map/jit(_take)/gather | solution.py:31
  138.4 72.9 %all-gather.4.cloned.1.call-done = f32[3,10,2,8192]{3,2,1,0:T(2,128)} async-done(((f32[3,10,2,128]{3,2,1,0:T(2,128)}), f32[3,10,2,8192]{3,2,1,0:T(2,128)}) %all-gather.4.cloned.1.call-update) | async-done | bytes 1966096 | tf_op jit(solution)/shard_map/all_gather | solution.py:30
  211.4 26.3 %copy.92 = f32[3,10,2,8192]{1,2,3,0:T(2,128)} copy(f32[3,10,2,8192]{3,2,1,0:T(2,128)} %all-gather.4.cloned.1.call-done) | data formatting | bytes 3932160 | tf_op jit(solution)/shard_map/all_gather | solution.py:30
  237.6 10.0 %gather_fusion = f32[128,3,10,2]{2,3,1,0:T(2,128)} fusion(f32[3,10,2,8192]{1,2,3,0:T(2,128)} %copy.92, s32[1024]{0:T(1024)S(1)} %pad_clamp_fusion), kind=kCustom, calls=%fused_computation.2 | custom fusion | bytes 61952 | tf_op jit(solution)/shard_map/jit(_take)/gather | solution.py:31
  247.7 1.5 bitcast_select_fusion
  251.2 1.3 fusion.20
  253.1 1.3 collective-permute-start.10
  254.6 3.1 collective-permute-start.8
  257.7 1.4 collective-permute-start.9
  260.1 1.3 collective-permute-start.11
  261.4 10.5 %collective-permute-done.8 = f32[2,10,32,2]{3,2,1,0:T(8,128)S(1)} collective-permute-done((f32[2,10,32,2]{3,2,1,0:T(8,128)S(1)}, f32[2,10,32,2]{3,2,1,0:T(8,128)S(1)}, u32[]{:S(2)}, u32[]{:S(2)}) %collective-permute-start.8) | collective-permute-done | bytes 5152 | tf_op jit(solution)/shard_map/ppermute | solution.py:17
  271.9 2.8 collective-permute-done.9
  275.4 67.0 %all-gather.8.cloned.1.call-done = f32[2,10,2,8192]{3,2,1,0:T(2,128)} async-done(((f32[2,10,2,128]{3,2,1,0:T(2,128)}), f32[2,10,2,8192]{3,2,1,0:T(2,128)}) %all-gather.8.cloned.1.call-update) | async-done | bytes 1310736 | tf_op jit(solution)/shard_map/all_gather | solution.py:30
  342.5 17.9 %copy.97 = f32[2,10,2,8192]{1,2,3,0:T(2,128)} copy(f32[2,10,2,8192]{3,2,1,0:T(2,128)} %all-gather.8.cloned.1.call-done) | data formatting | bytes 2621440 | tf_op jit(solution)/shard_map/all_gather | solution.py:30
  360.3 6.7 %gather_fusion.2 = f32[128,2,10,2]{2,3,1,0:T(2,128)S(1)} fusion(f32[2,10,2,8192]{1,2,3,0:T(2,128)} %copy.97, s32[1024]{0:T(1024)S(1)} %pad_clamp_fusion), kind=kCustom, calls=%fused_computation.1.clone | custom fusion | bytes 41472 | tf_op jit(solution)/shard_map/jit(_take)/gather | solution.py:31
  (58 shorter events, 15.0 us)
Async XLA Ops:
  7.2 105.6 %all-gather.6.cloned.1.call-start = ((), (), s32[]{:S(2)}) async-start(), calls=%async_computation.1 | async-start | bytes 1331200 | tf_op jit(solution)/shard_map/all_gather | solution.py:30
  8.7 202.6 %all-gather.4.cloned.1.call-start = ((), (), s32[]{:S(2)}) async-start(), calls=%async_computation | async-start | bytes 1996800 | tf_op jit(solution)/shard_map/all_gather | solution.py:30
  11.3 331.1 %all-gather.8.cloned.1.call-start = ((), (), s32[]{:S(2)}) async-start(), calls=%async_computation.2 | async-start | bytes 1331200 | tf_op jit(solution)/shard_map/all_gather | solution.py:30
  11.4 238.7 %collective-permute-start.4 = (f32[3,10,2,128]{3,2,1,0:T(2,128)S(1)}, f32[3,10,2,128]{3,2,1,0:T(2,128)}, u32[]{:S(2)}, u32[]{:S(2)}) collective-permute-start(f32[3,10,2,128]{3,2,1,0:T(2,128)S(1)} %get-tuple-element.15), channel_id=1, source_target_pairs={{0,1},{1,2},{2,3},{4,5},{5,6},{6,7},{8,9},{9,10},{10,11},{12,13},{... | collective-permute-start | bytes 92168 | tf_op jit(solution)/shard_map/ppermute | solution.py:17
  13.7 123.9 %collective-permute-start.6 = (f32[2,10,2,128]{3,2,1,0:T(2,128)S(1)}, f32[2,10,2,128]{3,2,1,0:T(2,128)}, u32[]{:S(2)}, u32[]{:S(2)}) collective-permute-start(f32[2,10,2,128]{3,2,1,0:T(2,128)S(1)} %get-tuple-element.29), channel_id=1, source_target_pairs={{0,1},{1,2},{2,3},{4,5},{5,6},{6,7},{8,9},{9,10},{10,11},{12,13},{... | collective-permute-start | bytes 61448 | tf_op jit(solution)/shard_map/ppermute | solution.py:17
  17.8 119.9 %copy-start = (f32[10,32,128]{2,1,0:T(8,128)S(1)}, f32[10,32,128]{2,1,0:T(8,128)}, u32[]{:S(2)}) copy-start(f32[10,32,128]{2,1,0:T(8,128)} %param.13) | copy-start | bytes 491524
  17.8 119.8 %copy-start.1 = (f32[10,32,128]{2,1,0:T(8,128)S(1)}, f32[10,32,128]{2,1,0:T(8,128)}, u32[]{:S(2)}) copy-start(f32[10,32,128]{2,1,0:T(8,128)} %param.12) | copy-start | bytes 491524
  17.8 229.9 %collective-permute-start.5 = (f32[3,10,2,128]{1,2,0,3:T(2,128)S(1)}, f32[3,10,2,128]{1,2,0,3:T(2,128)}, u32[]{:S(2)}, u32[]{:S(2)}) collective-permute-start(f32[3,10,2,128]{1,2,0,3:T(2,128)S(1)} %copy.93), channel_id=1, source_target_pairs={{1,0},{2,1},{3,2},{5,4},{6,5},{7,6},{9,8},{10,9},{11,10},{13,12},{... | collective-permute-start | bytes 92168 | tf_op jit(solution)/shard_map/ppermute | solution.py:19
  20.5 18.0 %collective-permute-start.2 = (f32[2,10,32,2]{3,2,1,0:T(8,128)S(1)}, f32[2,10,32,2]{3,2,1,0:T(8,128)S(1)}, u32[]{:S(2)}, u32[]{:S(2)}) collective-permute-start(f32[2,10,32,2]{3,2,1,0:T(8,128)S(1)} %get-tuple-element.25), channel_id=1, source_target_pairs={{0,4},{4,8},{8,12},{12,16},{16,20},{20,24},{24,28},{28,32},{32,36}... | collective-permute-start | bytes 15368 | tf_op jit(solution)/shard_map/ppermute | solution.py:17
  23.5 19.0 %collective-permute-start.3 = (f32[2,10,32,2]{3,2,1,0:T(8,128)S(1)}, f32[2,10,32,2]{3,2,1,0:T(8,128)S(1)}, u32[]{:S(2)}, u32[]{:S(2)}) collective-permute-start(f32[2,10,32,2]{3,2,1,0:T(8,128)S(1)} %get-tuple-element.26), channel_id=1, source_target_pairs={{4,0},{8,4},{12,8},{16,12},{20,16},{24,20},{28,24},{32,28},{36,32}... | collective-permute-start | bytes 15368 | tf_op jit(solution)/shard_map/ppermute | solution.py:19
  28.1 0.7 copy-start.4
  38.5 27.0 %collective-permute-start = (f32[3,10,32,2]{3,2,1,0:T(8,128)S(1)}, f32[3,10,32,2]{3,2,1,0:T(8,128)S(1)}, u32[]{:S(2)}, u32[]{:S(2)}) collective-permute-start(f32[3,10,32,2]{3,2,1,0:T(8,128)S(1)} %get-tuple-element.13), channel_id=1, source_target_pairs={{0,4},{4,8},{8,12},{12,16},{16,20},{20,24},{24,28},{28,32},{32,36}... | collective-permute-start | bytes 23048 | tf_op jit(solution)/shard_map/ppermute | solution.py:17
  42.5 24.3 %collective-permute-start.1 = (f32[3,10,32,2]{3,2,1,0:T(8,128)S(1)}, f32[3,10,32,2]{3,2,1,0:T(8,128)S(1)}, u32[]{:S(2)}, u32[]{:S(2)}) collective-permute-start(f32[3,10,32,2]{3,2,1,0:T(8,128)S(1)} %get-tuple-element.14), channel_id=1, source_target_pairs={{4,0},{8,4},{12,8},{16,12},{20,16},{24,20},{28,24},{32,28},{36,32}... | collective-permute-start | bytes 23048 | tf_op jit(solution)/shard_map/ppermute | solution.py:19
  65.5 72.1 %collective-permute-start.7 = (f32[2,10,2,128]{3,2,1,0:T(2,128)S(1)}, f32[2,10,2,128]{3,2,1,0:T(2,128)S(1)}, u32[]{:S(2)}, u32[]{:S(2)}) collective-permute-start(f32[2,10,2,128]{3,2,1,0:T(2,128)S(1)} %get-tuple-element.30), channel_id=1, source_target_pairs={{1,0},{2,1},{3,2},{5,4},{6,5},{7,6},{9,8},{10,9},{11,10},{13,12},{... | collective-permute-start | bytes 61448 | tf_op jit(solution)/shard_map/ppermute | solution.py:19
  130.6 117.1 %copy-start.6 = (f32[3]{0:T(128)S(1)}, f32[3]{0:T(128)}, u32[]{:S(2)}) copy-start(f32[3]{0:T(128)} %constant.55.clone) | copy-start | bytes 40
  130.6 119.4 %copy-start.2 = (f32[10,32,128]{2,1,0:T(8,128)S(1)}, f32[10,32,128]{2,1,0:T(8,128)}, u32[]{:S(2)}) copy-start(f32[10,32,128]{2,1,0:T(8,128)} %param.15) | copy-start | bytes 491524
  130.6 119.4 %copy-start.3 = (f32[10,32,128]{2,1,0:T(8,128)S(1)}, f32[10,32,128]{2,1,0:T(8,128)}, u32[]{:S(2)}) copy-start(f32[10,32,128]{2,1,0:T(8,128)} %param.14) | copy-start | bytes 491524
  130.6 120.3 %copy-start.5 = (f32[10]{0:T(128)S(1)}, f32[10]{0:T(128)}, u32[]{:S(2)}) copy-start(f32[10]{0:T(128)} %param.18) | copy-start | bytes 124
  253.1 114.1 %collective-permute-start.10 = (f32[2,10,2,128]{3,2,1,0:T(2,128)S(1)}, f32[2,10,2,128]{3,2,1,0:T(2,128)S(1)}, u32[]{:S(2)}, u32[]{:S(2)}) collective-permute-start(f32[2,10,2,128]{3,2,1,0:T(2,128)S(1)} %get-tuple-element.21), channel_id=1, source_target_pairs={{0,1},{1,2},{2,3},{4,5},{5,6},{6,7},{8,9},{9,10},{10,11},{12,13},{... | collective-permute-start | bytes 61448 | tf_op jit(solution)/shard_map/ppermute | solution.py:17
  254.6 17.3 %collective-permute-start.8 = (f32[2,10,32,2]{3,2,1,0:T(8,128)S(1)}, f32[2,10,32,2]{3,2,1,0:T(8,128)S(1)}, u32[]{:S(2)}, u32[]{:S(2)}) collective-permute-start(f32[2,10,32,2]{3,2,1,0:T(8,128)S(1)} %get-tuple-element.19), channel_id=1, source_target_pairs={{0,4},{4,8},{8,12},{12,16},{16,20},{20,24},{24,28},{28,32},{32,36}... | collective-permute-start | bytes 15368 | tf_op jit(solution)/shard_map/ppermute | solution.py:17
  257.7 17.0 %collective-permute-start.9 = (f32[2,10,32,2]{3,2,1,0:T(8,128)S(1)}, f32[2,10,32,2]{3,2,1,0:T(8,128)S(1)}, u32[]{:S(2)}, u32[]{:S(2)}) collective-permute-start(f32[2,10,32,2]{3,2,1,0:T(8,128)S(1)} %get-tuple-element.20), channel_id=1, source_target_pairs={{4,0},{8,4},{12,8},{16,12},{20,16},{24,20},{28,24},{32,28},{36,32}... | collective-permute-start | bytes 15368 | tf_op jit(solution)/shard_map/ppermute | solution.py:19
  260.1 107.2 %collective-permute-start.11 = (f32[2,10,2,128]{3,2,1,0:T(2,128)S(1)}, f32[2,10,2,128]{3,2,1,0:T(2,128)S(1)}, u32[]{:S(2)}, u32[]{:S(2)}) collective-permute-start(f32[2,10,2,128]{3,2,1,0:T(2,128)S(1)} %get-tuple-element.22), channel_id=1, source_target_pairs={{1,0},{2,1},{3,2},{5,4},{6,5},{7,6},{9,8},{10,9},{11,10},{13,12},{... | collective-permute-start | bytes 61448 | tf_op jit(solution)/shard_map/ppermute | solution.py:19
Sparse Core Ops, SparseCore 0:
  11.4 101.2 all-gather.5
  116.7 94.5 all-gather.3
  253.3 89.1 all-gather.7
where the time goes:
time: 381 us; the launch traced here: 375 us
  waiting for transfers between devices  225 us (59%)
  local copies, waits for them, and re-layouts  90.7 us (24%)
  starting transfers between devices  25 us (7%)
  other arithmetic  19.9 us (5%)
  between operations  14 us (4%)
    all_gather x3, waiting for transfers between devices, extend(): gathered = lax.all_gather(rows, 'lon', axis=3, tiled=True)  183 us
    all_gather x3, local copies, waits for them, and re-layouts, extend(): gathered = lax.all_gather(rows, 'lon', axis=3, tiled=True)  62 us
    ppermute x6, waiting for transfers between devices, with_halo(): lax.ppermute(tail, axis, [(i, (i + 1) % count) for i in range(ends)])  39.3 us
    gather x5, local copies, waits for them, and re-layouts, extend(): picked = jnp.take(gathered, partner, axis=3)  23.9 us
    ppermute x6, starting transfers between devices, with_halo(): lax.ppermute(tail, axis, [(i, (i + 1) % count) for i in range(ends)])  17.5 us
  transfers between devices with their start and end apart: 15, of which 7 were waited for; matrix products, arithmetic and copies ran while one was open for 28% of the time, Pallas kernels for 0%

commit v1 on v0

v1 whole, which is shorter than its diff:
```python
import functools

import jax
import jax.numpy as jnp
from jax import lax
from jax.experimental import pallas as pl
from jax.experimental.pallas import tpu as pltpu
from jax.sharding import PartitionSpec as P

STEPS = 2
GROUP = 4
LANES = 128
SLOT = 12
F32 = jnp.float32
MESH = pl.DeviceIdType.MESH
VMEM = pl.BlockSpec(memory_space=pltpu.VMEM)
SMEM = pl.BlockSpec(memory_space=pltpu.SMEM)


def roll(x, shift, axis=1):
    return pltpu.roll(x, shift, axis)


def pack(temp, salt, u_vel, v_vel, land, cols, north, south):
    levels, height, _ = temp.shape
    lane = lax.broadcasted_iota(jnp.int32, (height, LANES), 1)

    def level(l, held):
        base = l * SLOT
        t, s, v = temp[l], salt[l], v_vel[l]
        o = land[l].astype(F32)
        here = lane - base
        held = jnp.where((here >= 0) & (here < 4), roll(t, base + 2), held)
        held = jnp.where((here >= 4) & (here < 8), roll(s, base + 6), held)
        held = jnp.where((here >= 8) & (here < 10), roll(u_vel[l], base + 9), held)
        held = jnp.where((here >= 10) & (here < 12), roll(o, base + 11), held)
        for ref, lo, edge in ((north, height - 2, height - 1), (south, 0, 0)):
            ref[pl.ds(l, 1)] = t[lo : lo + 1]
            ref[pl.ds(levels + l, 1)] = t[lo + 1 : lo + 2]
            ref[pl.ds(2 * levels + l, 1)] = s[lo : lo + 1]
            ref[pl.ds(3 * levels + l, 1)] = s[lo + 1 : lo + 2]
            ref[pl.ds(4 * levels + l, 1)] = v[edge : edge + 1]
            ref[pl.ds(5 * levels + l, 1)] = o[edge : edge + 1]
        return held

    cols[...] = lax.fori_loop(0, levels, level, jnp.zeros((height, LANES), F32))


def pack_kernel(temp, salt, u_vel, v_vel, land, cols, north, south):
    pack(temp, salt, u_vel, v_vel, land, cols, north, south)


def exchange_kernel(branch, nlon, nlat, cols, north, south, west, east, below, above, send, recv):
    lon, lat = lax.axis_index("lon"), lax.axis_index("lat")
    top = lat == nlat - 1
    right, left = lax.rem(lon + 1, nlon), lax.rem(lon + nlon - 1, nlon)
    folds = [lax.rem(branch * GROUP - 1 + o - lon + 2 * nlon, nlon) for o in range(GROUP + 1)]
    barrier = pltpu.get_barrier_semaphore()

    def greet(a, b):
        pl.semaphore_signal(barrier, inc=1, device_id=(a, b), device_id_type=MESH)

    def copy(src, dst, slot, a, b):
        return pltpu.make_async_remote_copy(
            src_ref=src, dst_ref=dst, send_sem=send.at[slot], recv_sem=recv.at[slot], device_id=(a, b), device_id_type=MESH
        )

    def stay(o):
        return pltpu.make_async_copy(north, above.at[o], recv.at[3 + o])

    greet(right, lat)
    greet(left, lat)
    count = 2

    @pl.when(lat > 0)
    def _():
        greet(lon, lat - 1)

    @pl.when(lat < nlat - 1)
    def _():
        greet(lon, lat + 1)

    for f in folds:

        @pl.when(top & (f != lon))
        def _():
            greet(f, lat)

        count += (top & (f != lon)).astype(jnp.int32)
    count += (lat > 0).astype(jnp.int32) + (lat < nlat - 1).astype(jnp.int32)
    pl.semaphore_wait(barrier, count)

    for o, f in enumerate(folds):

        @pl.when(top & (f != lon))
        def _():
            copy(north, above.at[o], 3 + o, f, lat).start()

        @pl.when(top & (f == lon))
        def _():
            stay(o).start()

    to_right = copy(cols, west, 0, right, lat)
    to_left = copy(cols, east, 1, left, lat)
    to_right.start()
    to_left.start()
    to_north = copy(north, below, 2, lon, lax.rem(lat + 1, nlat))
    to_south = copy(south, above.at[0], 3, lon, lax.rem(lat + nlat - 1, nlat))

    @pl.when(lat < nlat - 1)
    def _():
        to_north.start()

    @pl.when(lat > 0)
    def _():
        copy_south(south, above, send, recv, lon, lat, nlat).start()

    to_right.wait()
    to_left.wait()

    @pl.when(lat > 0)
    def _():
        to_north.wait_recv()
        copy_south(south, above, send, recv, lon, lat, nlat).wait_send()

    @pl.when(lat < nlat - 1)
    def _():
        to_north.wait_send()
        to_south.wait_recv()

    for o, f in enumerate(folds):

        @pl.when(top & (f != lon))
        def _():
            copy(north, above.at[o], 3 + o, f, lat).wait()

        @pl.when(top & (f == lon))
        def _():
            stay(o).wait()


def copy_south(south, above, send, recv, lon, lat, nlat):
    return pltpu.make_async_remote_copy(
        src_ref=south,
        dst_ref=above.at[0],
        send_sem=send.at[4 + GROUP],
        recv_sem=recv.at[3],
        device_id=(lon, lax.rem(lat + nlat - 1, nlat)),
        device_id_type=MESH,
    )


def exchange(branch, nlon, nlat):
    def call(cols, north, south):
        rows = jax.ShapeDtypeStruct(north.shape, F32)
        side = jax.ShapeDtypeStruct(cols.shape, F32)
        return pl.pallas_call(
            functools.partial(exchange_kernel, branch, nlon, nlat),
            out_shape=(side, side, rows, jax.ShapeDtypeStruct((GROUP + 1,) + north.shape, F32)),
            in_specs=[VMEM] * 3,
            out_specs=[VMEM] * 4,
            scratch_shapes=[pltpu.SemaphoreType.DMA((5 + GROUP,)), pltpu.SemaphoreType.DMA((4 + GROUP,))],
            compiler_params=pltpu.CompilerParams(collective_id=1 + branch, has_side_effects=True),
            name=f"exchange_{branch}",
        )(cols, north, south)

    return call


def flux(c0, c1, before, after, speed, opened, diffuse):
    return opened * (speed * ((7.0 * (c0 + c1) - (before + after)) * (1.0 / 24.0)) - diffuse * (c1 - c0))


def step_kernel(
    nlon, nlat, temp, salt, u_vel, v_vel, land, partner, kappa_h, kappa_v, cols, west, east, below, above,
    temp_out, salt_out, cols_out, north_out, south_out, t_ext, s_ext, v_ext, o_ext, under, over,
):
    levels, height, _ = temp.shape
    lon, lat = lax.axis_index("lon"), lax.axis_index("lat")
    top = lat == nlat - 1
    shift = (partner[0] + lon * LANES) & (nlon * LANES - 1)
    tile, offset = shift // LANES, shift & (LANES - 1)
    near = lax.rem(tile, GROUP)
    lane_r = lax.broadcasted_iota(jnp.int32, north_out.shape, 1)
    order = jnp.where(top, (offset - lane_r) & (LANES - 1), lane_r)
    first = jnp.take_along_axis(above[jnp.where(top, near + 1, 0)], order, axis=1)
    second = jnp.take_along_axis(above[near], order, axis=1)
    over[...] = jnp.where(jnp.logical_or(jnp.logical_not(top), lane_r <= offset), first, second)
    under[...] = jnp.where(lat > 0, below[...], 0.0)
    flip = jnp.where(top, 1, 0)
    sign = jnp.where(top, -1.0, 1.0)
    end = height + 8

    def lay(l, carry):
        t_ext[l, 8:end] = temp[l]
        s_ext[l, 8:end] = salt[l]
        v_ext[l, 8:end] = v_vel[l]
        o_ext[l, 8:end] = land[l].astype(F32)
        for ref, j in ((t_ext, 0), (s_ext, 2)):
            ref[l, 6:7] = under[pl.ds(j * levels + l, 1)]
            ref[l, 7:8] = under[pl.ds((j + 1) * levels + l, 1)]
            ref[l, end : end + 1] = over[pl.ds((j + flip) * levels + l, 1)]
            ref[l, end + 1 : end + 2] = over[pl.ds((j + 1 - flip) * levels + l, 1)]
        v_ext[l, 7:8] = under[pl.ds(4 * levels + l, 1)]
        v_ext[l, end : end + 1] = over[pl.ds(4 * levels + l, 1)] * sign
        o_ext[l, 7:8] = under[pl.ds(5 * levels + l, 1)]
        o_ext[l, end : end + 1] = over[pl.ds(5 * levels + l, 1)]
        return carry

    lax.fori_loop(0, levels, lay, 0)

    lane = lax.broadcasted_iota(jnp.int32, (height, LANES), 1)
    mine, theirs, other = cols[...], west[...], east[...]
    kappas = lax.fori_loop(
        0, levels, lambda l, k: jnp.where((lane >= l * SLOT) & (lane < (l + 1) * SLOT), kappa_h[l], k), jnp.zeros_like(mine)
    )

    def west_face(back):
        def at(x, place):
            return roll(x, (LANES - place) % LANES) if place else x

        speed = at(theirs, 8 - back) + at(mine, 9 - back)
        opened = at(theirs, 10 - back) * at(mine, 11 - back)
        return flux(at(theirs, 1), at(mine, 2), theirs, at(mine, 3), speed, opened, kappas)

    faces = (west_face(0), west_face(4))

    def level(l, carry):
        base = l * SLOT
        diffuse = kappa_h[l]
        down, up = jnp.maximum(l - 1, 0), jnp.minimum(l + 1, levels - 1)
        k_down = jnp.where(l > 0, kappa_v[down], 0.0)
        k_up = jnp.where(l < levels - 1, kappa_v[jnp.minimum(l, levels - 2)], 0.0)
        own = pl.ds(8, height)
        u, o = u_vel[l], o_ext[l, own]
        u_next = jnp.where(lane == LANES - 1, roll(other, 118 - base), roll(u, LANES - 1))
        o_next = jnp.where(lane == LANES - 1, roll(other, 116 - base), roll(o, LANES - 1))
        speed_x, open_x = u + u_next, o * o_next
        tall = height + 8
        speed_y = v_ext[l, pl.ds(7, tall)] + v_ext[l, pl.ds(8, tall)]
        open_y = o_ext[l, pl.ds(7, tall)] * o_ext[l, pl.ds(8, tall)]
        lift = k_up * (o * o_ext[up, own])
        drop = k_down * (o * o_ext[down, own])
        for ext, out, face, back in ((t_ext, temp_out, faces[0], 0), (s_ext, salt_out, faces[1], 4)):
            c = ext[l, own]
            before = jnp.where(lane == 0, roll(theirs, 127 - back - base), roll(c, 1))
            next1 = jnp.where(lane == LANES - 1, roll(other, 125 - back - base), roll(c, LANES - 1))
            next2 = jnp.where(lane >= LANES - 2, roll(other, 124 - back - base), roll(c, LANES - 2))
            flux_x = flux(c, next1, before, next2, speed_x, open_x, diffuse)
            flux_w = jnp.where(lane == 0, roll(face, lax.rem(LANES - back - base + LANES, LANES)), roll(flux_x, 1))
            flux_y = flux(
                ext[l, pl.ds(7, tall)], ext[l, pl.ds(8, tall)], ext[l, pl.ds(6, tall)], ext[l, pl.ds(9, tall)],
                speed_y, open_y, diffuse,
            )
            flux_n = roll(flux_y, tall - 1, 0)
            gain = lift * (ext[up, own] - c) - drop * (c - ext[down, own])
            out[l] = c + o * (gain - (flux_x - flux_w) - (flux_n[:height] - flux_y[:height]))
        return carry

    lax.fori_loop(0, levels, level, 0)
    pack(temp_out, salt_out, u_vel, v_vel, land, cols_out, north_out, south_out)


def local(nlon, nlat, temp, salt, u_vel, v_vel, land_sea, partner, kappa_h, kappa_v):
    levels, height, width = temp.shape
    block = jax.ShapeDtypeStruct(temp.shape, F32)
    side = jax.ShapeDtypeStruct((height, width), F32)
    rows = jax.ShapeDtypeStruct((64, width), F32)
    edges = pl.pallas_call(
        pack_kernel, out_shape=(side, rows, rows), in_specs=[VMEM] * 5, out_specs=[VMEM] * 3, name="edges"
    )(temp, salt, u_vel, v_vel, land_sea)
    shift = (partner[0] + lax.axis_index("lon") * LANES) & (nlon * LANES - 1)
    branch = shift // (LANES * GROUP)
    branches = [exchange(b, nlon, nlat) for b in range(nlon // GROUP)]
    extended = pltpu.VMEM((levels, height + 24, width), F32)

    def step(i, state):
        t, s, cols, north, south = state
        west, east, below, above = lax.switch(branch, branches, cols, north, south)
        return tuple(
            pl.pallas_call(
                functools.partial(step_kernel, nlon, nlat),
                out_shape=(block, block, side, rows, rows),
                in_specs=[VMEM] * 5 + [SMEM] * 3 + [VMEM] * 5,
                out_specs=[VMEM] * 5,
                scratch_shapes=[extended] * 4 + [pltpu.VMEM((64, width), F32)] * 2,
                name="step",
            )(t, s, u_vel, v_vel, land_sea, partner, kappa_h, kappa_v, cols, west, east, below, above)
        )

    state = lax.fori_loop(0, STEPS, step, (temp, salt) + tuple(edges))
    return state[0], state[1]


def solution(mesh):
    field = P(None, "lat", "lon")
    return jax.shard_map(
        functools.partial(local, mesh.shape["lon"], mesh.shape["lat"]),
        mesh=mesh,
        in_specs=(field,) * 5 + (P("lon"), P(), P()),
        out_specs=(field, field),
        check_vma=False,
    )
```

time: 381 us -> 43.6 us (0.11)
  the two profiles are of different devices: /device:TPU:2 before, /device:TPU:59 now
where the time goes in v1:
time: 43.6 us; the launch traced here: 43.4 us
  Pallas kernels  36.5 us (84%)
  local copies, waits for them, and re-layouts  5.97 us (14%)
  between operations  0.77 us (2%)
    pallas_call x2, Pallas kernels, call(): pl.pallas_call(functools.partial(exchange_kernel, branch, nlon, nlat), ou...  26.8 us
    pallas_call x2, Pallas kernels, step(): pl.pallas_call(functools.partial(step_kernel, nlon, nlat), out_shape=(blo...  8.89 us
    unnamed x20, local copies, waits for them, and re-layouts  3.3 us
    while x6, local copies, waits for them, and re-layouts  2.67 us

profile of v1, /device:TPU:59, one launch (start us, length us, event | category | flops | bytes accessed | tf_op | source)
XLA Modules:
  0.0 43.4 jit_solution(16126818900106865048)
XLA Ops:
  0.6 0.0 copy-start.5
  0.6 0.0 copy-start.4
  0.6 1.0 %copy.99.salt = f32[10,32,128]{2,1,0:T(8,128)S(1)} copy(f32[10,32,128]{2,1,0:T(8,128)} %param.27) | data formatting | bytes 327680
  1.6 0.0 copy-done.5
  1.6 0.0 copy-start.2
  1.6 0.0 copy-start.3
  1.6 0.0 copy-start.6
  1.7 0.7 %copy-done.6 = s32[128]{0:T(128)S(1)} copy-done((s32[128]{0:T(128)S(1)}, s32[128]{0:T(128)}, u32[]{:S(2)}) %copy-start.6) | copy-done | bytes 536
  2.4 0.0 copy-done.4
  2.4 0.2 copy-done.2
  2.6 0.1 copy-done.3
  2.7 0.8 %edges.1 = (f32[32,128]{1,0:T(8,128)S(1)}, f32[64,128]{1,0:T(8,128)S(1)}, f32[64,128]{1,0:T(8,128)S(1)}) custom-call(f32[10,32,128]{2,1,0:T(8,128)S(1)} %copy.98.temp, f32[10,32,128]{2,1,0:T(8,128)S(1)} %copy.99.salt, f32[10,32,128]{2,1,0:T(8,128)S(1)} %copy-done.2, f32[10,32,128]{2,1,0:T(8,128)S(1)} %copy-done.3, s32[10,32,128]{2,1,0:T(8,128)S(1)} %copy-done.4), custom_call_target="tpu_custom_call" | custom-call | tf_op jit(solution)/shard_map/edges/pallas_call | solution.py:269
  3.5 0.0 copy-start.7
  3.5 0.0 copy-start.8
  3.5 0.6 %copy-done.7 = f32[10]{0:T(128)S(1)} copy-done((f32[10]{0:T(128)S(1)}, f32[10]{0:T(128)}, u32[]{:S(2)}) %copy-start.7) | copy-done | bytes 64
  4.2 0.0 copy-done.8
  4.2 38.5 %while.20 = (s32[]{:T(128)}, f32[10,32,128]{2,1,0:T(8,128)S(1)}, f32[10,32,128]{2,1,0:T(8,128)S(1)}, f32[32,128]{1,0:T(8,128)S(1)}, f32[64,128]{1,0:T(8,128)S(1)...) while((s32[]{:T(128)}, f32[10,32,128]{2,1,0:T(8,128)S(1)}, ...), condition=%wide.region_17.18_spmd, body=%wide.region_0.17_spmd.sunk | while | flops 2 | bytes 688293 | solution.py:291
  4.2 0.7 %copy.101.temp = f32[10,32,128]{2,1,0:T(8,128)} copy(f32[10,32,128]{2,1,0:T(8,128)S(1)} %get-tuple-element.511) | data formatting | bytes 327680 | tf_op jit(solution)/shard_map/while
  4.8 0.7 %copy.102.salt = f32[10,32,128]{2,1,0:T(8,128)} copy(f32[10,32,128]{2,1,0:T(8,128)S(1)} %get-tuple-element.512) | data formatting | bytes 327680 | tf_op jit(solution)/shard_map/while
  5.5 15.1 %conditional.2 = ((f32[32,128]{1,0:T(8,128)S(1)}, f32[32,128]{1,0:T(8,128)S(1)}, f32[64,128]{1,0:T(8,128)S(1)}, f32[5,64,128]{2,1,0:T(8,128)S(1)})) conditional(s32[]{:T(128)} %get-tuple-element.530, (f32[32,128]{1,0:T(8,128)S(1)}, f32[64,128]{1,0:T(8,128)S(1)}, f32[64,128]{1,0:T(8,128)S(1)}) %tuple.78, ...), branch_computations={%region_1.1_spmd, %region_2.2_spmd, %region_3.3_spmd, %region_4.4_... | conditional | bytes 8 | solution.py:279
  5.5 15.0 %exchange_0.1 = (f32[32,128]{1,0:T(8,128)S(1)}, f32[32,128]{1,0:T(8,128)S(1)}, f32[64,128]{1,0:T(8,128)S(1)}, f32[5,64,128]{2,1,0:T(8,128)S(1)}) custom-call(f32[32,128]{1,0:T(8,128)S(1)} %get-tuple-element.226.cols, f32[64,128]{1,0:T(8,128)S(1)} %get-tuple-element.227.north, f32[64,128]{1,0:T(8,128)S(1)} %get-tuple-element.228.south), custom_call_target="tpu_custom_call" | custom-call | tf_op jit(solution)/shard_map/while/body/eval_jaxpr/cond/branch_0_fun/exchange_0/pallas_call | solution.py:157
  20.6 4.4 %step.3 = (f32[10,32,128]{2,1,0:T(8,128)S(1)}, f32[10,32,128]{2,1,0:T(8,128)S(1)}, f32[32,128]{1,0:T(8,128)S(1)}, f32[64,128]{1,0:T(8,128)S(1)}, f32[64,128]{1,0:T(8,128)S(1)}) custom-call(f32[10,32,128]{2,1,0:T(8,128)} %copy.101.temp, f32[10,32,128]{2,1,0:T(8,128)} %copy.102.salt, f32[10,32,128]{2,1,0:T(8,128)S(1)} %get-tuple-element.531.u_vel, ...), custom_call_target="tpu_custom_call" | custom-call | tf_op jit(solution)/shard_map/while/body/eval_jaxpr/step/pallas_call | solution.py:281
  25.0 0.7 %copy.101.temp = f32[10,32,128]{2,1,0:T(8,128)} copy(f32[10,32,128]{2,1,0:T(8,128)S(1)} %get-tuple-element.511) | data formatting | bytes 327680 | tf_op jit(solution)/shard_map/while
  25.7 0.7 %copy.102.salt = f32[10,32,128]{2,1,0:T(8,128)} copy(f32[10,32,128]{2,1,0:T(8,128)S(1)} %get-tuple-element.512) | data formatting | bytes 327680 | tf_op jit(solution)/shard_map/while
  26.4 11.8 %conditional.2 = ((f32[32,128]{1,0:T(8,128)S(1)}, f32[32,128]{1,0:T(8,128)S(1)}, f32[64,128]{1,0:T(8,128)S(1)}, f32[5,64,128]{2,1,0:T(8,128)S(1)})) conditional(s32[]{:T(128)} %get-tuple-element.530, (f32[32,128]{1,0:T(8,128)S(1)}, f32[64,128]{1,0:T(8,128)S(1)}, f32[64,128]{1,0:T(8,128)S(1)}) %tuple.78, ...), branch_computations={%region_1.1_spmd, %region_2.2_spmd, %region_3.3_spmd, %region_4.4_... | conditional | bytes 8 | solution.py:279
  26.4 11.8 %exchange_0.1 = (f32[32,128]{1,0:T(8,128)S(1)}, f32[32,128]{1,0:T(8,128)S(1)}, f32[64,128]{1,0:T(8,128)S(1)}, f32[5,64,128]{2,1,0:T(8,128)S(1)}) custom-call(f32[32,128]{1,0:T(8,128)S(1)} %get-tuple-element.226.cols, f32[64,128]{1,0:T(8,128)S(1)} %get-tuple-element.227.north, f32[64,128]{1,0:T(8,128)S(1)} %get-tuple-element.228.south), custom_call_target="tpu_custom_call" | custom-call | tf_op jit(solution)/shard_map/while/body/eval_jaxpr/cond/branch_0_fun/exchange_0/pallas_call | solution.py:157
  38.2 4.4 %step.3 = (f32[10,32,128]{2,1,0:T(8,128)S(1)}, f32[10,32,128]{2,1,0:T(8,128)S(1)}, f32[32,128]{1,0:T(8,128)S(1)}, f32[64,128]{1,0:T(8,128)S(1)}, f32[64,128]{1,0:T(8,128)S(1)}) custom-call(f32[10,32,128]{2,1,0:T(8,128)} %copy.101.temp, f32[10,32,128]{2,1,0:T(8,128)} %copy.102.salt, f32[10,32,128]{2,1,0:T(8,128)S(1)} %get-tuple-element.531.u_vel, ...), custom_call_target="tpu_custom_call" | custom-call | tf_op jit(solution)/shard_map/while/body/eval_jaxpr/step/pallas_call | solution.py:281
  42.7 0.0 copy-start
  42.7 0.0 copy-start.1
  42.7 0.6 %copy-done = f32[10,32,128]{2,1,0:T(8,128)} copy-done((f32[10,32,128]{2,1,0:T(8,128)}, f32[10,32,128]{2,1,0:T(8,128)S(1)}, u32[]{:S(2)}) %copy-start) | copy-done | bytes 163864
  43.3 0.1 copy-done.1
  (3 shorter events, 0.0 us)
Async XLA Ops:
  0.6 1.0 %copy-start.5 = (f32[10,32,128]{2,1,0:T(8,128)S(1)}, f32[10,32,128]{2,1,0:T(8,128)}, u32[]{:S(2)}) copy-start(f32[10,32,128]{2,1,0:T(8,128)} %param.26) | copy-start | bytes 491524
  0.6 1.8 %copy-start.4 = (s32[10,32,128]{2,1,0:T(8,128)S(1)}, s32[10,32,128]{2,1,0:T(8,128)}, u32[]{:S(2)}) copy-start(s32[10,32,128]{2,1,0:T(8,128)} %land.1) | copy-start | bytes 491524
  1.6 1.0 %copy-start.2 = (f32[10,32,128]{2,1,0:T(8,128)S(1)}, f32[10,32,128]{2,1,0:T(8,128)}, u32[]{:S(2)}) copy-start(f32[10,32,128]{2,1,0:T(8,128)} %u_vel.1) | copy-start | bytes 491524
  1.6 1.0 %copy-start.3 = (f32[10,32,128]{2,1,0:T(8,128)S(1)}, f32[10,32,128]{2,1,0:T(8,128)}, u32[]{:S(2)}) copy-start(f32[10,32,128]{2,1,0:T(8,128)} %v_vel.1) | copy-start | bytes 491524
  1.6 0.7 %copy-start.6 = (s32[128]{0:T(128)S(1)}, s32[128]{0:T(128)}, u32[]{:S(2)}) copy-start(s32[128]{0:T(128)} %param.31) | copy-start | bytes 1540
  3.5 0.7 %copy-start.7 = (f32[10]{0:T(128)S(1)}, f32[10]{0:T(128)}, u32[]{:S(2)}) copy-start(f32[10]{0:T(128)} %param.32) | copy-start | bytes 124
  3.5 0.7 %copy-start.8 = (f32[9]{0:T(128)S(1)}, f32[9]{0:T(128)}, u32[]{:S(2)}) copy-start(f32[9]{0:T(128)} %param.33) | copy-start | bytes 112
  42.7 0.7 %copy-start = (f32[10,32,128]{2,1,0:T(8,128)}, f32[10,32,128]{2,1,0:T(8,128)S(1)}, u32[]{:S(2)}) copy-start(f32[10,32,128]{2,1,0:T(8,128)S(1)} %get-tuple-element.303) | copy-start | bytes 491524
  42.7 0.7 %copy-start.1 = (f32[10,32,128]{2,1,0:T(8,128)}, f32[10,32,128]{2,1,0:T(8,128)S(1)}, u32[]{:S(2)}) copy-start(f32[10,32,128]{2,1,0:T(8,128)S(1)} %get-tuple-element.302) | copy-start | bytes 491524

commit v2 on v0

v2 whole, which is shorter than its diff:
```python
import functools

import jax
import jax.numpy as jnp
from jax import lax
from jax.experimental import pallas as pl
from jax.experimental.pallas import tpu as pltpu
from jax.sharding import PartitionSpec as P

STEPS = 2
WIDE = 8
LANES = 128
SLOT = 12
EDGE = 64
MOVING = 40
F32 = jnp.float32
MESH = pl.DeviceIdType.MESH
HALO = 8


def roll(x, shift, axis=1):
    return pltpu.roll(x, shift, axis)


def flux(c0, c1, before, after, speed, opened, diffuse):
    return opened * (speed * ((7.0 * (c0 + c1) - (before + after)) * (1.0 / 24.0)) - diffuse * (c1 - c0))


def kernel(
    nlon, nlat, temp, salt, u_vel, v_vel, land, partner, kappa_h, kappa_v, temp_out, salt_out,
    t_ext, s_ext, v_ext, o_ext, u_own, land_own, t_new, s_new, cols, north, south, relay, west, east, below, above,
    group0, group1, across0, across1, under, over, face_t, face_s,
    load_sem, out_sem, send, recv, group_send, group_recv, across_send, across_recv,
):
    group, across = (group0, group1), (across0, across1)
    levels, height, _ = temp.shape
    end = HALO + height
    lon, lat = lax.axis_index("lon"), lax.axis_index("lat")
    top = lat == nlat - 1
    right, left = lax.rem(lon + 1, nlon), lax.rem(lon + nlon - 1, nlon)
    place, far = lax.rem(lon, WIDE), lon // WIDE
    groups = nlon // WIDE

    def in_group(k):
        return far * WIDE + lax.rem(place + k, WIDE)

    def in_across(k):
        return lax.rem(far + k, groups) * WIDE + place

    loads = [
        pltpu.make_async_copy(src, dst, load_sem.at[i])
        for i, (src, dst) in enumerate(
            (
                (temp, t_ext.at[0, :, pl.ds(HALO, height)]),
                (salt, s_ext.at[0, :, pl.ds(HALO, height)]),
                (v_vel, v_ext.at[:, pl.ds(HALO, height)]),
                (land, land_own),
                (u_vel, u_own),
            )
        )
    ]
    for load in loads:
        load.start()

    barrier = pltpu.get_barrier_semaphore()

    def greet(a, b):
        pl.semaphore_signal(barrier, inc=1, device_id=(a, b), device_id_type=MESH)

    @pl.when(top)
    def _():
        for k in range(1, WIDE):
            greet(in_group(k), lat)
        for k in range(1, groups):
            greet(in_across(k), lat)

    greet(right, lat)
    greet(left, lat)

    @pl.when(lat > 0)
    def _():
        greet(lon, lat - 1)

    @pl.when(lat < nlat - 1)
    def _():
        greet(lon, lat + 1)

    expected = 2 + jnp.where(lat > 0, 1, 0) + jnp.where(top, WIDE + groups - 2, 1)

    def remote(src, dst, sent, got, a, b):
        return pltpu.make_async_remote_copy(
            src_ref=src, dst_ref=dst, send_sem=sent, recv_sem=got, device_id=(a, b), device_id_type=MESH
        )

    def rows(step):
        return pl.ds(0, EDGE if step == 0 else MOVING)

    def to_right(step):
        return remote(cols.at[step], west.at[step], send.at[step, 0], recv.at[step, 0], right, lat)

    def to_left(step):
        return remote(cols.at[step], east.at[step], send.at[step, 1], recv.at[step, 1], left, lat)

    def to_north(step):
        return remote(
            north.at[step, rows(step)], below.at[step, rows(step)], send.at[step, 2], recv.at[step, 2], lon, lax.rem(lat + 1, nlat)
        )

    def to_south(step):
        return remote(
            south.at[step, rows(step)], above.at[step, rows(step)], send.at[step, 3], recv.at[step, 3],
            lon, lax.rem(lat + nlat - 1, nlat),
        )

    def to_group(step, k):
        return remote(
            north.at[step, rows(step)], group[step].at[k, rows(step)], group_send.at[step, k], group_recv.at[step, k], in_group(k), lat
        )

    def to_across(step, k):
        return remote(
            relay.at[step, rows(step)], across[step].at[k, rows(step)], across_send.at[step, k], across_recv.at[step, k],
            in_across(k), lat,
        )

    def pack_north(step):
        def level(l, carry):
            for j, (ref, row) in enumerate(((t_ext, end - 2), (t_ext, end - 1), (s_ext, end - 2), (s_ext, end - 1))):
                north[step, pl.ds(j * levels + l, 1)] = ref[step, l, pl.ds(row, 1)]
            if step == 0:
                north[step, pl.ds(4 * levels + l, 1)] = v_ext[l, pl.ds(end - 1, 1)]
                north[step, pl.ds(5 * levels + l, 1)] = land_own[l, pl.ds(height - 1, 1)].astype(F32)
            return carry

        lax.fori_loop(0, levels, level, 0)

    def pack_south(step):
        def level(l, carry):
            for j, (ref, row) in enumerate(((t_ext, HALO), (t_ext, HALO + 1), (s_ext, HALO), (s_ext, HALO + 1))):
                south[step, pl.ds(j * levels + l, 1)] = ref[step, l, pl.ds(row, 1)]
            if step == 0:
                south[step, pl.ds(4 * levels + l, 1)] = v_ext[l, pl.ds(HALO, 1)]
                south[step, pl.ds(5 * levels + l, 1)] = land_own[l, pl.ds(0, 1)].astype(F32)
            return carry

        lax.fori_loop(0, levels, level, 0)

    lane = lax.broadcasted_iota(jnp.int32, (height, LANES), 1)
    own = pl.ds(HALO, height)

    def pack_cols(step):
        def level(l, held):
            base = l * SLOT
            here = lane - base
            held = jnp.where((here >= 0) & (here < 4), roll(t_ext[step, l, own], base + 2), held)
            held = jnp.where((here >= 4) & (here < 8), roll(s_ext[step, l, own], base + 6), held)
            held = jnp.where((here >= 8) & (here < 10), roll(u_own[l], base + 9), held)
            return jnp.where((here >= 10) & (here < 12), roll(o_ext[l, own], base + 11), held)

        cols[step] = lax.fori_loop(0, levels, level, jnp.zeros((height, LANES), F32))

    def lay_south(step):
        under[...] = jnp.where(lat > 0, below[step], 0.0)

        def level(l, carry):
            for ref, j in ((t_ext, 0), (s_ext, 2)):
                ref[step, l, pl.ds(HALO - 2, 1)] = under[pl.ds(j * levels + l, 1)]
                ref[step, l, pl.ds(HALO - 1, 1)] = under[pl.ds((j + 1) * levels + l, 1)]
            if step == 0:
                v_ext[l, pl.ds(HALO - 1, 1)] = under[pl.ds(4 * levels + l, 1)]
                o_ext[l, pl.ds(HALO - 1, 1)] = under[pl.ds(5 * levels + l, 1)]
            return carry

        lax.fori_loop(0, levels, level, 0)

    def lay_north(step, source, folded):
        flip, sign = (1, -1.0) if folded else (0, 1.0)

        def level(l, carry):
            for ref, j in ((t_ext, 0), (s_ext, 2)):
                ref[step, l, pl.ds(end, 1)] = source[pl.ds((j + flip) * levels + l, 1)]
                ref[step, l, pl.ds(end + 1, 1)] = source[pl.ds((j + 1 - flip) * levels + l, 1)]
            if step == 0:
                v_ext[l, pl.ds(end, 1)] = source[pl.ds(4 * levels + l, 1)] * sign
                o_ext[l, pl.ds(end, 1)] = source[pl.ds(5 * levels + l, 1)]
            return carry

        lax.fori_loop(0, levels, level, 0)

    def make_faces(step):
        mine, theirs = cols[step], west[step]
        kappas = lax.fori_loop(
            0,
            levels,
            lambda l, k: jnp.where((lane >= l * SLOT) & (lane < (l + 1) * SLOT), kappa_h[l], k),
            jnp.zeros((height, LANES), F32),
        )

        def at(x, p):
            return roll(x, (LANES - p) % LANES) if p else x

        for ref, back in ((face_t, 0), (face_s, 4)):
            speed = at(theirs, 8 - back) + at(mine, 9 - back)
            opened = at(theirs, 10 - back) * at(mine, 11 - back)
            ref[...] = flux(at(theirs, 1), at(mine, 2), theirs, at(mine, 3), speed, opened, kappas)

    def advance(step, row, count, t_out, s_out, shift):
        here, tall = pl.ds(HALO + row, count), count + 8
        span = lane[:count]
        side = pl.ds(row, count)
        theirs, other = west[step, side], east[step, side]
        faces = (face_t[side], face_s[side])

        def rise(k):
            return pl.ds(HALO + row - 1 + k, tall)

        def level(l, carry):
            base = l * SLOT
            diffuse = kappa_h[l]
            down, up = jnp.maximum(l - 1, 0), jnp.minimum(l + 1, levels - 1)
            k_down = jnp.where(l > 0, kappa_v[down], 0.0)
            k_up = jnp.where(l < levels - 1, kappa_v[jnp.minimum(l, levels - 2)], 0.0)
            u, o = u_own[l, side], o_ext[l, here]
            u_next = jnp.where(span == LANES - 1, roll(other, 118 - base), roll(u, LANES - 1))
            o_next = jnp.where(span == LANES - 1, roll(other, 116 - base), roll(o, LANES - 1))
            speed_x, open_x = u + u_next, o * o_next
            speed_y = v_ext[l, rise(0)] + v_ext[l, rise(1)]
            open_y = o_ext[l, rise(0)] * o_ext[l, rise(1)]
            lift = k_up * (o * o_ext[up, here])
            drop = k_down * (o * o_ext[down, here])
            for ext, out, face, back in ((t_ext, t_out, faces[0], 0), (s_ext, s_out, faces[1], 4)):
                c = ext[step, l, here]
                before = jnp.where(span == 0, roll(theirs, 127 - back - base), roll(c, 1))
                next1 = jnp.where(span == LANES - 1, roll(other, 125 - back - base), roll(c, LANES - 1))
                next2 = jnp.where(span >= LANES - 2, roll(other, 124 - back - base), roll(c, LANES - 2))
                flux_x = flux(c, next1, before, next2, speed_x, open_x, diffuse)
                flux_w = jnp.where(span == 0, roll(face, lax.rem(2 * LANES - back - base, LANES)), roll(flux_x, 1))
                flux_y = flux(
                    ext[step, l, rise(0)], ext[step, l, rise(1)], ext[step, l, rise(-1)], ext[step, l, rise(2)],
                    speed_y, open_y, diffuse,
                )
                flux_n = roll(flux_y, tall - 1, 0)
                gain = lift * (ext[step, up, here] - c) - drop * (c - ext[step, down, here])
                out[l, pl.ds(shift + row, count)] = c + o * (
                    gain - (flux_x - flux_w) - (flux_n[:count] - flux_y[:count])
                )
            return carry

        lax.fori_loop(0, levels, level, 0)

    shift = (partner[0] + lon * LANES) & (nlon * LANES - 1)
    tile, offset = shift // LANES, shift & (LANES - 1)
    tile_far, tile_place = tile // WIDE, lax.rem(tile, WIDE)
    edge_lane = lax.broadcasted_iota(jnp.int32, (EDGE, LANES), 1)
    order = (offset - edge_lane) & (LANES - 1)
    near_part = edge_lane <= offset
    borrow0 = jnp.where(tile_place < place, 1, 0)
    borrow1 = jnp.where(tile_place - 1 < place, 1, 0)

    def assemble(step):
        first = jnp.take_along_axis(group[step][lax.rem(2 * place - tile_place + WIDE, WIDE)], order, axis=1)
        second = jnp.take_along_axis(group[step][lax.rem(2 * place - tile_place + 1 + WIDE, WIDE)], order, axis=1)
        relay[step] = jnp.where(near_part, first, second)

    def choose(step):
        from0 = across[step][lax.rem(2 * far - tile_far + borrow0 + 2 * groups, groups)]
        from1 = across[step][lax.rem(2 * far - tile_far + borrow1 + 2 * groups, groups)]
        over[...] = jnp.where(near_part, from0, from1)

    for load in loads[:4]:
        load.wait()
    pack_north(0)
    pack_south(0)
    pl.semaphore_wait(barrier, expected)

    @pl.when(top)
    def _():
        for k in range(1, WIDE):
            to_group(0, k).start()
        group[0][0] = north[0]

    @pl.when(lat < nlat - 1)
    def _():
        to_north(0).start()

    @pl.when(lat > 0)
    def _():
        to_south(0).start()

    loads[4].wait()

    def ocean(l, carry):
        o_ext[l, own] = land_own[l].astype(F32)
        return carry

    lax.fori_loop(0, levels, ocean, 0)

    for step in range(STEPS):
        last = step == STEPS - 1
        t_out, s_out, at = (t_new, s_new, 0) if last else (t_ext.at[step + 1], s_ext.at[step + 1], HALO)
        pack_cols(step)
        to_right(step).start()
        to_left(step).start()

        @pl.when(top)
        def _():
            for k in range(1, WIDE):
                to_group(step, k).wait_recv()
            assemble(step)
            for k in range(1, groups):
                to_across(step, k).start()
            across[step][0] = relay[step]

        @pl.when(lat > 0)
        def _():
            to_north(step).wait_recv()

        lay_south(step)

        @pl.when(lat < nlat - 1)
        def _():
            to_south(step).wait_recv()
            lay_north(step, above.at[step], False)

        to_right(step).wait_recv()
        to_left(step).wait_recv()
        make_faces(step)
        advance(step, 0, height, t_out, s_out, at)
        if not last:
            pack_south(step + 1)

            @pl.when(lat > 0)
            def _():
                to_south(step + 1).start()

        @pl.when(top)
        def _():
            for k in range(1, groups):
                to_across(step, k).wait_recv()
            choose(step)
            lay_north(step, over, True)
            advance(step, height - 8, 8, t_out, s_out, at)

        if not last:
            pack_north(step + 1)

            @pl.when(top)
            def _():
                for k in range(1, WIDE):
                    to_group(step + 1, k).start()
                group[step + 1][0] = north[step + 1]

            @pl.when(lat < nlat - 1)
            def _():
                to_north(step + 1).start()

    outs = [
        pltpu.make_async_copy(src, dst, out_sem.at[i]) for i, (src, dst) in enumerate(((t_new, temp_out), (s_new, salt_out)))
    ]
    for out in outs:
        out.start()
    for step in range(STEPS):
        to_right(step).wait_send()
        to_left(step).wait_send()

        @pl.when(lat < nlat - 1)
        def _():
            to_north(step).wait_send()

        @pl.when(lat > 0)
        def _():
            to_south(step).wait_send()

        @pl.when(top)
        def _():
            for k in range(1, WIDE):
                to_group(step, k).wait_send()
            for k in range(1, groups):
                to_across(step, k).wait_send()

    for out in outs:
        out.wait()


def local(nlon, nlat, temp, salt, u_vel, v_vel, land_sea, partner, kappa_h, kappa_v):
    levels, height, width = temp.shape
    block = jax.ShapeDtypeStruct(temp.shape, F32)
    anywhere = pl.BlockSpec(memory_space=pl.ANY)
    numbers = pl.BlockSpec(memory_space=pltpu.SMEM)
    groups = nlon // WIDE

    def room(*shape):
        return pltpu.VMEM(shape, F32)

    tall = height + 24
    return pl.pallas_call(
        functools.partial(kernel, nlon, nlat),
        out_shape=(block, block),
        in_specs=[anywhere] * 5 + [numbers] * 3,
        out_specs=[anywhere] * 2,
        scratch_shapes=[
            room(STEPS, levels, tall, width),
            room(STEPS, levels, tall, width),
            room(levels, tall, width),
            room(levels, tall, width),
            room(levels, height, width),
            pltpu.VMEM((levels, height, width), jnp.int32),
            room(levels, height, width),
            room(levels, height, width),
            room(STEPS, height, width),
            room(STEPS, EDGE, width),
            room(STEPS, EDGE, width),
            room(STEPS, EDGE, width),
            room(STEPS, height, width),
            room(STEPS, height, width),
            room(STEPS, EDGE, width),
            room(STEPS, EDGE, width),
            room(WIDE, EDGE, width),
            room(WIDE, EDGE, width),
            room(groups, EDGE, width),
            room(groups, EDGE, width),
            room(EDGE, width),
            room(EDGE, width),
            room(height, width),
            room(height, width),
            pltpu.SemaphoreType.DMA((5,)),
            pltpu.SemaphoreType.DMA((2,)),
            pltpu.SemaphoreType.DMA((STEPS, 4)),
            pltpu.SemaphoreType.DMA((STEPS, 4)),
            pltpu.SemaphoreType.DMA((STEPS, WIDE)),
            pltpu.SemaphoreType.DMA((STEPS, WIDE)),
            pltpu.SemaphoreType.DMA((STEPS, groups)),
            pltpu.SemaphoreType.DMA((STEPS, groups)),
        ],
        compiler_params=pltpu.CompilerParams(collective_id=0, has_side_effects=True, vmem_limit_bytes=60 << 20),
        name="tracer_steps",
    )(temp, salt, u_vel, v_vel, land_sea, partner, kappa_h, kappa_v)


def solution(mesh):
    field = P(None, "lat", "lon")
    return jax.shard_map(
        functools.partial(local, mesh.shape["lon"], mesh.shape["lat"]),
        mesh=mesh,
        in_specs=(field,) * 5 + (P("lon"), P(), P()),
        out_specs=(field, field),
        check_vma=False,
    )
```

time: 381 us -> 38.8 us (0.10)
  the two profiles are of different devices: /device:TPU:2 before, /device:TPU:9 now
where the time goes in v2:
time: 38.8 us; the launch traced here: 38.6 us
  Pallas kernels  35.7 us (92%)
  local copies, waits for them, and re-layouts  2.3 us (6%)
  between operations  0.65 us (2%)
    pallas_call x1, Pallas kernels, local(): pl.pallas_call(functools.partial(kernel, nlon, nlat), out_shape=(block, b...  35.7 us
    unnamed x4, local copies, waits for them, and re-layouts  2.3 us

profile of v2, /device:TPU:9, one launch (start us, length us, event | category | flops | bytes accessed | tf_op | source)
XLA Modules:
  0.0 38.6 jit_solution(7987848895844591705)
XLA Ops:
  0.6 35.7 %tracer_steps.1 = (f32[10,32,128]{2,1,0:T(8,128)}, f32[10,32,128]{2,1,0:T(8,128)}) custom-call(f32[10,32,128]{2,1,0:T(8,128)} %temp.1, f32[10,32,128]{2,1,0:T(8,128)} %salt.1, f32[10,32,128]{2,1,0:T(8,128)} %u_vel.1, f32[10,32,128]{2,1,0:T(8,128)} %v_vel.1, s32[10,32,128]{2,1,0:T(8,128)} %land.1, s32[128]{0:T(128)} %partner.1, f32[10]{0:T(128)} %kappa_h.1, ...), custom_call_target="tpu_custom_call" | custom-call | tf_op jit(solution)/shard_map/tracer_steps/pallas_call | solution.py:396
  36.3 0.0 copy-start
  36.3 1.6 %copy.12 = f32[10,32,128]{2,1,0:T(8,128)} copy(f32[10,32,128]{2,1,0:T(8,128)} %get-tuple-element.4) | data formatting | bytes 327680
  38.0 0.0 copy-done
  38.0 0.7 %copy.13 = f32[10,32,128]{2,1,0:T(8,128)} copy(f32[10,32,128]{2,1,0:T(8,128)S(1)} %copy-done) | data formatting | bytes 327680
Async XLA Ops:
  36.3 1.6 %copy-start = (f32[10,32,128]{2,1,0:T(8,128)S(1)}, f32[10,32,128]{2,1,0:T(8,128)}, u32[]{:S(2)}) copy-start(f32[10,32,128]{2,1,0:T(8,128)} %get-tuple-element.5) | copy-start | bytes 491524

commit v3 on v2

v3 whole, which is shorter than its diff:
```python
import functools

import jax
import jax.numpy as jnp
from jax import lax
from jax.experimental import pallas as pl
from jax.experimental.pallas import tpu as pltpu
from jax.sharding import PartitionSpec as P

STEPS = 2
WIDE = 8
LANES = 128
SLOT = 12
EDGE = 32
UNROLL = 5
F32 = jnp.float32
MESH = pl.DeviceIdType.MESH
HALO = 8


def roll(x, shift, axis=1):
    return pltpu.roll(x, shift, axis)


def flux(c0, c1, before, after, speed, opened, diffuse):
    return opened * (speed * ((7.0 * (c0 + c1) - (before + after)) * (1.0 / 24.0)) - diffuse * (c1 - c0))


def kernel(
    nlon, nlat, temp, salt, u_vel, v_vel, land, partner, kappa_h, kappa_v, temp_out, salt_out,
    t_ext, s_ext, v_ext, o_ext, u_own, land_own, land_rows, cols, north, south, relay, west, east, below, above,
    near00, near01, near10, near11, far00, far01, far10, far11, under, over, face_t, face_s,
    load_sem, row_sem, send, recv, near_send, near_recv, far_send, far_recv,
):
    hop_near, hop_far = ((near00, near01), (near10, near11)), ((far00, far01), (far10, far11))
    levels, height, _ = temp.shape
    end = HALO + height
    lon, lat = lax.axis_index("lon"), lax.axis_index("lat")
    top = lat == nlat - 1
    right, left = lax.rem(lon + 1, nlon), lax.rem(lon + nlon - 1, nlon)
    place, far = lax.rem(lon, WIDE), lon // WIDE
    groups = nlon // WIDE

    def farthest_first(count):
        return sorted(range(1, count), key=lambda k: -min(k, count - k))

    def in_group(k):
        return far * WIDE + lax.rem(place + k, WIDE)

    def in_across(k):
        return lax.rem(far + k, groups) * WIDE + place

    def row_copy(field, row, dst, i):
        return pltpu.make_async_copy(field.at[:, row], dst, row_sem.at[i])

    first_rows = [
        row_copy(temp, height - 2, north.at[0, 0, pl.ds(0, levels)], 0),
        row_copy(temp, height - 1, north.at[0, 0, pl.ds(levels, levels)], 1),
        row_copy(v_vel, height - 1, north.at[0, 0, pl.ds(2 * levels, levels)], 2),
        row_copy(salt, height - 2, north.at[0, 1, pl.ds(0, levels)], 3),
        row_copy(salt, height - 1, north.at[0, 1, pl.ds(levels, levels)], 4),
        row_copy(land, height - 1, land_rows.at[0], 5),
        row_copy(temp, 0, south.at[0, 0, pl.ds(0, levels)], 6),
        row_copy(temp, 1, south.at[0, 0, pl.ds(levels, levels)], 7),
        row_copy(v_vel, 0, south.at[0, 0, pl.ds(2 * levels, levels)], 8),
        row_copy(salt, 0, south.at[0, 1, pl.ds(0, levels)], 9),
        row_copy(salt, 1, south.at[0, 1, pl.ds(levels, levels)], 10),
        row_copy(land, 0, land_rows.at[1], 11),
    ]
    for copy in first_rows:
        copy.start()

    loads = [
        pltpu.make_async_copy(src, dst, load_sem.at[i])
        for i, (src, dst) in enumerate(
            (
                (temp, t_ext.at[0, :, pl.ds(HALO, height)]),
                (salt, s_ext.at[0, :, pl.ds(HALO, height)]),
                (v_vel, v_ext.at[:, pl.ds(HALO, height)]),
                (land, land_own),
                (u_vel, u_own),
            )
        )
    ]
    for load in loads:
        load.start()

    barrier = pltpu.get_barrier_semaphore()

    def greet(a, b):
        pl.semaphore_signal(barrier, inc=1, device_id=(a, b), device_id_type=MESH)

    @pl.when(top)
    def _():
        for k in range(1, WIDE):
            greet(in_group(k), lat)
        for k in range(1, groups):
            greet(in_across(k), lat)

    greet(right, lat)
    greet(left, lat)

    @pl.when(lat > 0)
    def _():
        greet(lon, lat - 1)

    @pl.when(lat < nlat - 1)
    def _():
        greet(lon, lat + 1)

    expected = 2 + jnp.where(lat > 0, 1, 0) + jnp.where(top, WIDE + groups - 2, 1)

    def remote(src, dst, sent, got, a, b):
        return pltpu.make_async_remote_copy(
            src_ref=src, dst_ref=dst, send_sem=sent, recv_sem=got, device_id=(a, b), device_id_type=MESH
        )

    def rows(step):
        return pl.ds(0, (3 if step == 0 else 2) * levels)

    def to_right(step):
        return remote(cols.at[step], west.at[step], send.at[step, 0], recv.at[step, 0], right, lat)

    def to_left(step):
        return remote(cols.at[step], east.at[step], send.at[step, 1], recv.at[step, 1], left, lat)

    def to_north(step):
        return remote(
            north.at[step, :, rows(step)], below.at[step, :, rows(step)], send.at[step, 2], recv.at[step, 2],
            lon, lax.rem(lat + 1, nlat),
        )

    def to_south(step):
        return remote(
            south.at[step, :, rows(step)], above.at[step, :, rows(step)], send.at[step, 3], recv.at[step, 3],
            lon, lax.rem(lat + nlat - 1, nlat),
        )

    def hop(step, tracer, near, k):
        message = (north if near == (tracer == 0) else relay).at[step, tracer, rows(step)]
        slots, sent, got, to = (
            (hop_near, near_send, near_recv, in_group) if near else (hop_far, far_send, far_recv, in_across)
        )
        return remote(
            message, slots[step][tracer].at[k, rows(step)], sent.at[step, tracer, k], got.at[step, tracer, k], to(k), lat
        )

    def peers(near):
        return farthest_first(WIDE if near else groups)

    def first_hop(step):
        for k in range(max(WIDE, groups)):
            for tracer, near in ((0, True), (1, False)):
                if k < len(peers(near)):
                    hop(step, tracer, near, peers(near)[k]).start()
        hop_near[step][0][0] = north[step, 0]
        hop_far[step][1][0] = north[step, 1]

    def pack_rows(step, ref, row):
        def level(l, carry):
            for tracer, ext in enumerate((t_ext, s_ext)):
                for i in range(2):
                    ref[step, tracer, pl.ds(i * levels + l, 1)] = ext[step, l, pl.ds(row + i, 1)]
            return carry

        lax.fori_loop(0, levels, level, 0, unroll=UNROLL)

    lane = lax.broadcasted_iota(jnp.int32, (height, LANES), 1)
    own = pl.ds(HALO, height)

    def pack_cols(step):
        def level(l, held):
            base = l * SLOT
            here = lane - base
            held = jnp.where((here >= 0) & (here < 4), roll(t_ext[step, l, own], base + 2), held)
            held = jnp.where((here >= 4) & (here < 8), roll(s_ext[step, l, own], base + 6), held)
            held = jnp.where((here >= 8) & (here < 10), roll(u_own[l], base + 9), held)
            return jnp.where((here >= 10) & (here < 12), roll(o_ext[l, own], base + 11), held)

        cols[step] = lax.fori_loop(0, levels, level, jnp.zeros((height, LANES), F32), unroll=UNROLL)

    def lay(step, source, row, still, flip, sign):
        def level(l, carry):
            for tracer, ext in enumerate((t_ext, s_ext)):
                ext[step, l, pl.ds(row, 1)] = source[tracer, pl.ds(flip * levels + l, 1)]
                ext[step, l, pl.ds(row + 1, 1)] = source[tracer, pl.ds((1 - flip) * levels + l, 1)]
            if step == 0:
                v_ext[l, pl.ds(still, 1)] = source[0, pl.ds(2 * levels + l, 1)] * sign
                o_ext[l, pl.ds(still, 1)] = source[1, pl.ds(2 * levels + l, 1)]
            return carry

        lax.fori_loop(0, levels, level, 0, unroll=UNROLL)

    def lay_south(step):
        under[...] = jnp.where(lat > 0, below[step], 0.0)
        lay(step, under, HALO - 2, HALO - 1, 0, 1.0)

    def lay_north(step, source, folded):
        lay(step, source, end, end, 1 if folded else 0, -1.0 if folded else 1.0)

    def make_faces(step):
        mine, theirs = cols[step], west[step]
        kappas = lax.fori_loop(
            0,
            levels,
            lambda l, k: jnp.where((lane >= l * SLOT) & (lane < (l + 1) * SLOT), kappa_h[l], k),
            jnp.zeros((height, LANES), F32),
        )

        def at(x, p):
            return roll(x, (LANES - p) % LANES) if p else x

        for ref, back in ((face_t, 0), (face_s, 4)):
            speed = at(theirs, 8 - back) + at(mine, 9 - back)
            opened = at(theirs, 10 - back) * at(mine, 11 - back)
            ref[...] = flux(at(theirs, 1), at(mine, 2), theirs, at(mine, 3), speed, opened, kappas)

    def advance(step, row, count, t_out, s_out, shift):
        here, tall = pl.ds(HALO + row, count), count + 8
        span = lane[:count]
        side = pl.ds(row, count)
        theirs, other = west[step, side], east[step, side]
        faces = (face_t[side], face_s[side])

        def rise(k):
            return pl.ds(HALO + row - 1 + k, tall)

        def level(l, carry):
            base = l * SLOT
            diffuse = kappa_h[l]
            down, up = jnp.maximum(l - 1, 0), jnp.minimum(l + 1, levels - 1)
            k_down = jnp.where(l > 0, kappa_v[down], 0.0)
            k_up = jnp.where(l < levels - 1, kappa_v[jnp.minimum(l, levels - 2)], 0.0)
            u, o = u_own[l, side], o_ext[l, here]
            u_next = jnp.where(span == LANES - 1, roll(other, 118 - base), roll(u, LANES - 1))
            o_next = jnp.where(span == LANES - 1, roll(other, 116 - base), roll(o, LANES - 1))
            speed_x, open_x = u + u_next, o * o_next
            speed_y = v_ext[l, rise(0)] + v_ext[l, rise(1)]
            open_y = o_ext[l, rise(0)] * o_ext[l, rise(1)]
            lift = k_up * (o * o_ext[up, here])
            drop = k_down * (o * o_ext[down, here])
            for ext, out, face, back in ((t_ext, t_out, faces[0], 0), (s_ext, s_out, faces[1], 4)):
                c = ext[step, l, here]
                before = jnp.where(span == 0, roll(theirs, 127 - back - base), roll(c, 1))
                next1 = jnp.where(span == LANES - 1, roll(other, 125 - back - base), roll(c, LANES - 1))
                next2 = jnp.where(span >= LANES - 2, roll(other, 124 - back - base), roll(c, LANES - 2))
                flux_x = flux(c, next1, before, next2, speed_x, open_x, diffuse)
                flux_w = jnp.where(span == 0, roll(face, lax.rem(2 * LANES - back - base, LANES)), roll(flux_x, 1))
                flux_y = flux(
                    ext[step, l, rise(0)], ext[step, l, rise(1)], ext[step, l, rise(-1)], ext[step, l, rise(2)],
                    speed_y, open_y, diffuse,
                )
                flux_n = roll(flux_y, tall - 1, 0)
                gain = lift * (ext[step, up, here] - c) - drop * (c - ext[step, down, here])
                out[l, pl.ds(shift + row, count)] = c + o * (
                    gain - (flux_x - flux_w) - (flux_n[:count] - flux_y[:count])
                )
            return carry

        lax.fori_loop(0, levels, level, 0, unroll=UNROLL)

    shift = (partner[0] + lon * LANES) & (nlon * LANES - 1)
    tile, offset = shift // LANES, shift & (LANES - 1)
    tile_far, tile_place = tile // WIDE, lax.rem(tile, WIDE)
    edge_lane = lax.broadcasted_iota(jnp.int32, (EDGE, LANES), 1)
    order = (offset - edge_lane) & (LANES - 1)
    near_part = edge_lane <= offset
    borrow0 = jnp.where(tile_place < place, 1, 0)
    borrow1 = jnp.where(tile_place - 1 < place, 1, 0)

    near_slots = [lax.rem(2 * place - tile_place + i + WIDE, WIDE) for i in range(2)]
    far_slots = [lax.rem(2 * far - tile_far + borrow + 2 * groups, groups) for borrow in (borrow0, borrow1)]

    def wait_hop(step, tracer, near):
        for k in peers(near):
            hop(step, tracer, near, k).wait_recv()

    def picked(step, tracer, near):
        slots, at = (hop_near, near_slots) if near else (hop_far, far_slots)
        return slots[step][tracer][at[0]], slots[step][tracer][at[1]]

    def second_hop(step):
        for tracer, near in ((0, True), (1, False)):
            wait_hop(step, tracer, near)
            first, second = picked(step, tracer, near)
            first = jnp.take_along_axis(first, order, axis=1)
            second = jnp.take_along_axis(second, order, axis=1)
            relay[step, tracer] = jnp.where(near_part, first, second)
            for k in peers(not near):
                hop(step, tracer, not near, k).start()
            (hop_far if near else hop_near)[step][tracer][0] = relay[step, tracer]

    def choose(step):
        for tracer, near in ((0, False), (1, True)):
            wait_hop(step, tracer, near)
            first, second = picked(step, tracer, near)
            over[tracer] = jnp.where(near_part, first, second)

    for copy in first_rows[:6]:
        copy.wait()
    north[0, 1, pl.ds(2 * levels, levels)] = land_rows[0].astype(F32)
    pl.semaphore_wait(barrier, expected)

    @pl.when(top)
    def _():
        first_hop(0)

    @pl.when(lat < nlat - 1)
    def _():
        to_north(0).start()

    for copy in first_rows[6:]:
        copy.wait()
    south[0, 1, pl.ds(2 * levels, levels)] = land_rows[1].astype(F32)

    @pl.when(lat > 0)
    def _():
        to_south(0).start()

    for load in loads:
        load.wait()

    def ocean(l, carry):
        o_ext[l, own] = land_own[l].astype(F32)
        return carry

    lax.fori_loop(0, levels, ocean, 0, unroll=UNROLL)

    for step in range(STEPS):
        last = step == STEPS - 1
        t_out, s_out, at = (temp_out, salt_out, 0) if last else (t_ext.at[step + 1], s_ext.at[step + 1], HALO)
        pack_cols(step)
        to_right(step).start()
        to_left(step).start()

        @pl.when(top)
        def _():
            second_hop(step)

        @pl.when(lat > 0)
        def _():
            to_north(step).wait_recv()

        lay_south(step)

        @pl.when(lat < nlat - 1)
        def _():
            to_south(step).wait_recv()
            lay_north(step, above.at[step], False)

        to_right(step).wait_recv()
        to_left(step).wait_recv()
        make_faces(step)
        advance(step, 0, height, t_out, s_out, at)
        if not last:
            pack_rows(step + 1, south, HALO)

            @pl.when(lat > 0)
            def _():
                to_south(step + 1).start()

        @pl.when(top)
        def _():
            choose(step)
            lay_north(step, over, True)
            advance(step, height - 8, 8, t_out, s_out, at)

        if not last:
            pack_rows(step + 1, north, end - 2)

            @pl.when(top)
            def _():
                first_hop(step + 1)

            @pl.when(lat < nlat - 1)
            def _():
                to_north(step + 1).start()

    for step in range(STEPS):
        to_right(step).wait_send()
        to_left(step).wait_send()

        @pl.when(lat < nlat - 1)
        def _():
            to_north(step).wait_send()

        @pl.when(lat > 0)
        def _():
            to_south(step).wait_send()

        @pl.when(top)
        def _():
            for tracer in range(2):
                for near in (True, False):
                    for k in peers(near):
                        hop(step, tracer, near, k).wait_send()


def local(nlon, nlat, temp, salt, u_vel, v_vel, land_sea, partner, kappa_h, kappa_v):
    levels, height, width = temp.shape
    block = jax.ShapeDtypeStruct(temp.shape, F32)
    anywhere = pl.BlockSpec(memory_space=pl.ANY)
    numbers = pl.BlockSpec(memory_space=pltpu.SMEM)
    groups = nlon // WIDE

    def room(*shape):
        return pltpu.VMEM(shape, F32)

    tall = height + 24
    return pl.pallas_call(
        functools.partial(kernel, nlon, nlat),
        out_shape=(block, block),
        in_specs=[anywhere] * 5 + [numbers] * 3,
        out_specs=[pl.BlockSpec(memory_space=pltpu.VMEM)] * 2,
        scratch_shapes=[
            room(STEPS, levels, tall, width),
            room(STEPS, levels, tall, width),
            room(levels, tall, width),
            room(levels, tall, width),
            room(levels, height, width),
            pltpu.VMEM((levels, height, width), jnp.int32),
            pltpu.VMEM((2, levels, width), jnp.int32),
            room(STEPS, height, width),
            room(STEPS, 2, EDGE, width),
            room(STEPS, 2, EDGE, width),
            room(STEPS, 2, EDGE, width),
            room(STEPS, height, width),
            room(STEPS, height, width),
            room(STEPS, 2, EDGE, width),
            room(STEPS, 2, EDGE, width),
            *[room(WIDE, EDGE, width)] * (2 * STEPS),
            *[room(groups, EDGE, width)] * (2 * STEPS),
            room(2, EDGE, width),
            room(2, EDGE, width),
            room(height, width),
            room(height, width),
            pltpu.SemaphoreType.DMA((5,)),
            pltpu.SemaphoreType.DMA((12,)),
            pltpu.SemaphoreType.DMA((STEPS, 4)),
            pltpu.SemaphoreType.DMA((STEPS, 4)),
            pltpu.SemaphoreType.DMA((STEPS, 2, WIDE)),
            pltpu.SemaphoreType.DMA((STEPS, 2, WIDE)),
            pltpu.SemaphoreType.DMA((STEPS, 2, groups)),
            pltpu.SemaphoreType.DMA((STEPS, 2, groups)),
        ],
        compiler_params=pltpu.CompilerParams(collective_id=0, has_side_effects=True, vmem_limit_bytes=60 << 20),
        name="tracer_steps",
    )(temp, salt, u_vel, v_vel, land_sea, partner, kappa_h, kappa_v)


def solution(mesh):
    field = P(None, "lat", "lon")
    return jax.shard_map(
        functools.partial(local, mesh.shape["lon"], mesh.shape["lat"]),
        mesh=mesh,
        in_specs=(field,) * 5 + (P("lon"), P(), P()),
        out_specs=(field, field),
        check_vma=False,
    )
```

time: 38.8 us -> 33.2 us (0.86)
  Pallas kernels: 35.7 us -> 30.1 us
    pallas_call x1, Pallas kernels: 35.7 us -> 30.1 us  [local(): pl.pallas_call(functools.partial(kernel, nlon, nlat), out_shape=(block, b...]
where the time goes in v3:
time: 33.2 us; the launch traced here: 33.1 us
  Pallas kernels  30.1 us (91%)
  local copies, waits for them, and re-layouts  2.3 us (7%)
  between operations  0.65 us (2%)
    pallas_call x1, Pallas kernels, local(): pl.pallas_call(functools.partial(kernel, nlon, nlat), out_shape=(block, b...  30.1 us
    unnamed x4, local copies, waits for them, and re-layouts  2.3 us

profile of v3, /device:TPU:9, one launch (start us, length us, event | category | flops | bytes accessed | tf_op | source)
XLA Modules:
  0.0 33.1 jit_solution(4498029675501384506)
XLA Ops:
  0.6 30.1 %tracer_steps.1 = (f32[10,32,128]{2,1,0:T(8,128)}, f32[10,32,128]{2,1,0:T(8,128)}) custom-call(f32[10,32,128]{2,1,0:T(8,128)} %temp.1, f32[10,32,128]{2,1,0:T(8,128)} %salt.1, f32[10,32,128]{2,1,0:T(8,128)} %u_vel.1, f32[10,32,128]{2,1,0:T(8,128)} %v_vel.1, s32[10,32,128]{2,1,0:T(8,128)} %land.1, s32[128]{0:T(128)} %partner.1, f32[10]{0:T(128)} %kappa_h.1, ...), custom_call_target="tpu_custom_call" | custom-call | tf_op jit(solution)/shard_map/tracer_steps/pallas_call | solution.py:410
  30.8 0.0 copy-start
  30.8 1.6 %copy.12 = f32[10,32,128]{2,1,0:T(8,128)} copy(f32[10,32,128]{2,1,0:T(8,128)} %get-tuple-element.4) | data formatting | bytes 327680
  32.4 0.0 copy-done
  32.4 0.7 %copy.13 = f32[10,32,128]{2,1,0:T(8,128)} copy(f32[10,32,128]{2,1,0:T(8,128)S(1)} %copy-done) | data formatting | bytes 327680
Async XLA Ops:
  30.8 1.6 %copy-start = (f32[10,32,128]{2,1,0:T(8,128)S(1)}, f32[10,32,128]{2,1,0:T(8,128)}, u32[]{:S(2)}) copy-start(f32[10,32,128]{2,1,0:T(8,128)} %get-tuple-element.5) | copy-start | bytes 491524

commit v4 on v3

--- a/solution.py
+++ b/solution.py
@@ -27,9 +27,11 @@
 
 
 def kernel(
-    nlon, nlat, temp, salt, u_vel, v_vel, land, partner, kappa_h, kappa_v, temp_out, salt_out,
+    nlon, nlat, temp, salt, u_vel, v_vel, land, partner_in, kappa_h_in, kappa_v_in, temp_out, salt_out,
+    partner, kappa_h, kappa_v,
     t_ext, s_ext, v_ext, o_ext, u_own, land_own, land_rows, cols, north, south, relay, west, east, below, above,
-    near00, near01, near10, near11, far00, far01, far10, far11, under, over, face_t, face_s,
+    near00, near01, near10, near11, far00, far01, far10, far11, under, over, under_top, mending,
+    face_t, face_s, kappas,
     load_sem, row_sem, send, recv, near_send, near_recv, far_send, far_recv,
 ):
     hop_near, hop_far = ((near00, near01), (near10, near11)), ((far00, far01), (far10, far11))
@@ -67,9 +69,6 @@
         row_copy(salt, 1, south.at[0, 1, pl.ds(levels, levels)], 10),
         row_copy(land, 0, land_rows.at[1], 11),
     ]
-    for copy in first_rows:
-        copy.start()
-
     loads = [
         pltpu.make_async_copy(src, dst, load_sem.at[i])
         for i, (src, dst) in enumerate(
@@ -79,12 +78,12 @@
                 (v_vel, v_ext.at[:, pl.ds(HALO, height)]),
                 (land, land_own),
                 (u_vel, u_own),
+                (partner_in, partner),
+                (kappa_h_in, kappa_h),
+                (kappa_v_in, kappa_v),
             )
         )
     ]
-    for load in loads:
-        load.start()
-
     barrier = pltpu.get_barrier_semaphore()
 
     def greet(a, b):
@@ -109,6 +108,9 @@
         greet(lon, lat + 1)
 
     expected = 2 + jnp.where(lat > 0, 1, 0) + jnp.where(top, WIDE + groups - 2, 1)
+
+    for copy in first_rows + loads:
+        copy.start()
 
     def remote(src, dst, sent, got, a, b):
         return pltpu.make_async_remote_copy(
@@ -174,56 +176,97 @@
             here = lane - base
             held = jnp.where((here >= 0) & (here < 4), roll(t_ext[step, l, own], base + 2), held)
             held = jnp.where((here >= 4) & (here < 8), roll(s_ext[step, l, own], base + 6), held)
-            held = jnp.where((here >= 8) & (here < 10), roll(u_own[l], base + 9), held)
-            return jnp.where((here >= 10) & (here < 12), roll(o_ext[l, own], base + 11), held)
-
-        cols[step] = lax.fori_loop(0, levels, level, jnp.zeros((height, LANES), F32), unroll=UNROLL)
-
-    def lay(step, source, row, still, flip, sign):
+            if step == 0:
+                held = jnp.where((here >= 8) & (here < 10), roll(u_own[l], base + 9), held)
+                held = jnp.where((here >= 10) & (here < 12), roll(o_ext[l, own], base + 11), held)
+            return held
+
+        cols[step] = lax.fori_loop(0, levels, level, cols[0] if step else jnp.zeros((height, LANES), F32), unroll=UNROLL)
+
+    def lay(step, source, row, still):
         def level(l, carry):
             for tracer, ext in enumerate((t_ext, s_ext)):
-                ext[step, l, pl.ds(row, 1)] = source[tracer, pl.ds(flip * levels + l, 1)]
-                ext[step, l, pl.ds(row + 1, 1)] = source[tracer, pl.ds((1 - flip) * levels + l, 1)]
+                for i in range(2):
+                    ext[step, l, pl.ds(row + i, 1)] = source[tracer, pl.ds(i * levels + l, 1)]
             if step == 0:
-                v_ext[l, pl.ds(still, 1)] = source[0, pl.ds(2 * levels + l, 1)] * sign
+                v_ext[l, pl.ds(still, 1)] = source[0, pl.ds(2 * levels + l, 1)]
                 o_ext[l, pl.ds(still, 1)] = source[1, pl.ds(2 * levels + l, 1)]
             return carry
 
         lax.fori_loop(0, levels, level, 0, unroll=UNROLL)
 
+    def crown():
+        above_own = jnp.zeros((2, LANES), F32)
+
+        def level(l, carry):
+            for step in range(STEPS):
+                t_ext[step, l, pl.ds(end, 2)] = above_own
+                s_ext[step, l, pl.ds(end, 2)] = above_own
+            v_ext[l, pl.ds(end, 2)] = above_own
+            o_ext[l, pl.ds(end, 2)] = above_own
+            under_top[0, pl.ds(l, 1)] = v_ext[l, pl.ds(end - 2, 1)]
+            under_top[1, pl.ds(l, 1)] = o_ext[l, pl.ds(end - 2, 1)]
+            under_top[2, pl.ds(l, 1)] = jnp.full((1, LANES), kappa_h[l], F32)
+            return carry
+
+        lax.fori_loop(0, levels, level, 0, unroll=UNROLL)
+
+    def mend(step):
+        first, second, still = pl.ds(0, levels), pl.ds(levels, levels), pl.ds(2 * levels, levels)
+        every = pl.ds(0, levels)
+        v2, o2, diffuse = under_top[0, every], under_top[1, every], under_top[2, every]
+        v1, o1 = north[0, 0, still], north[0, 1, still]
+        v_ghost, o_ghost = -over[0, 0, still], over[0, 1, still]
+        lower = o2 * o1 * (v2 + v1) * (-1.0 / 24.0)
+        speed, opened = v1 + v_ghost, o1 * o_ghost
+        for tracer in range(2):
+            c2, c1 = north[step, tracer, first], north[step, tracer, second]
+            g1, g2 = over[step, tracer, second], over[step, tracer, first]
+            missing = lower * g1
+            face = flux(c1, g1, c2, g2, speed, opened, diffuse)
+            mending[tracer, first] = o2 * missing
+            mending[tracer, second] = o1 * (face - missing)
+
+    def mend_rows(t_out, s_out, row):
+        def level(l, carry):
+            for tracer, out in enumerate((t_out, s_out)):
+                for i in range(2):
+                    here = pl.ds(row + i, 1)
+                    out[l, here] = out[l, here] - mending[tracer, pl.ds(i * levels + l, 1)]
+            return carry
+
+        lax.fori_loop(0, levels, level, 0, unroll=UNROLL)
+
     def lay_south(step):
         under[...] = jnp.where(lat > 0, below[step], 0.0)
-        lay(step, under, HALO - 2, HALO - 1, 0, 1.0)
-
-    def lay_north(step, source, folded):
-        lay(step, source, end, end, 1 if folded else 0, -1.0 if folded else 1.0)
-
-    def make_faces(step):
-        mine, theirs = cols[step], west[step]
-        kappas = lax.fori_loop(
+        lay(step, under, HALO - 2, HALO - 1)
+
+    def lay_kappas():
+        kappas[...] = lax.fori_loop(
             0,
             levels,
             lambda l, k: jnp.where((lane >= l * SLOT) & (lane < (l + 1) * SLOT), kappa_h[l], k),
             jnp.zeros((height, LANES), F32),
-        )
-
+            unroll=UNROLL,
+        )
+
+    def make_faces(step):
+        mine, theirs = cols[step], west[step]
         def at(x, p):
             return roll(x, (LANES - p) % LANES) if p else x
 
         for ref, back in ((face_t, 0), (face_s, 4)):
             speed = at(theirs, 8 - back) + at(mine, 9 - back)
             opened = at(theirs, 10 - back) * at(mine, 11 - back)
-            ref[...] = flux(at(theirs, 1), at(mine, 2), theirs, at(mine, 3), speed, opened, kappas)
-
-    def advance(step, row, count, t_out, s_out, shift):
-        here, tall = pl.ds(HALO + row, count), count + 8
-        span = lane[:count]
-        side = pl.ds(row, count)
-        theirs, other = west[step, side], east[step, side]
-        faces = (face_t[side], face_s[side])
+            ref[...] = flux(at(theirs, 1), at(mine, 2), theirs, at(mine, 3), speed, opened, kappas[...])
+
+    def advance(step, t_out, s_out, shift):
+        here, tall = own, height + 8
+        theirs, other = west[step], east[step]
+        faces = (face_t[...], face_s[...])
 
         def rise(k):
-            return pl.ds(HALO + row - 1 + k, tall)
+            return pl.ds(HALO - 1 + k, tall)
 
         def level(l, carry):
             base = l * SLOT
@@ -231,9 +274,9 @@
             down, up = jnp.maximum(l - 1, 0), jnp.minimum(l + 1, levels - 1)
             k_down = jnp.where(l > 0, kappa_v[down], 0.0)
             k_up = jnp.where(l < levels - 1, kappa_v[jnp.minimum(l, levels - 2)], 0.0)
-            u, o = u_own[l, side], o_ext[l, here]
-            u_next = jnp.where(span == LANES - 1, roll(other, 118 - base), roll(u, LANES - 1))
-            o_next = jnp.where(span == LANES - 1, roll(other, 116 - base), roll(o, LANES - 1))
+            u, o = u_own[l], o_ext[l, here]
+            u_next = jnp.where(lane == LANES - 1, roll(other, 118 - base), roll(u, LANES - 1))
+            o_next = jnp.where(lane == LANES - 1, roll(other, 116 - base), roll(o, LANES - 1))
             speed_x, open_x = u + u_next, o * o_next
             speed_y = v_ext[l, rise(0)] + v_ext[l, rise(1)]
             open_y = o_ext[l, rise(0)] * o_ext[l, rise(1)]
@@ -241,35 +284,21 @@
             drop = k_down * (o * o_ext[down, here])
             for ext, out, face, back in ((t_ext, t_out, faces[0], 0), (s_ext, s_out, faces[1], 4)):
                 c = ext[step, l, here]
-                before = jnp.where(span == 0, roll(theirs, 127 - back - base), roll(c, 1))
-                next1 = jnp.where(span == LANES - 1, roll(other, 125 - back - base), roll(c, LANES - 1))
-                next2 = jnp.where(span >= LANES - 2, roll(other, 124 - back - base), roll(c, LANES - 2))
+                before = jnp.where(lane == 0, roll(theirs, 127 - back - base), roll(c, 1))
+                next1 = jnp.where(lane == LANES - 1, roll(other, 125 - back - base), roll(c, LANES - 1))
+                next2 = jnp.where(lane >= LANES - 2, roll(other, 124 - back - base), roll(c, LANES - 2))
                 flux_x = flux(c, next1, before, next2, speed_x, open_x, diffuse)
-                flux_w = jnp.where(span == 0, roll(face, lax.rem(2 * LANES - back - base, LANES)), roll(flux_x, 1))
+                flux_w = jnp.where(lane == 0, roll(face, lax.rem(2 * LANES - back - base, LANES)), roll(flux_x, 1))
                 flux_y = flux(
                     ext[step, l, rise(0)], ext[step, l, rise(1)], ext[step, l, rise(-1)], ext[step, l, rise(2)],
                     speed_y, open_y, diffuse,
                 )
                 flux_n = roll(flux_y, tall - 1, 0)
                 gain = lift * (ext[step, up, here] - c) - drop * (c - ext[step, down, here])
-                out[l, pl.ds(shift + row, count)] = c + o * (
-                    gain - (flux_x - flux_w) - (flux_n[:count] - flux_y[:count])
-                )
+                out[l, pl.ds(shift, height)] = c + o * (gain - (flux_x - flux_w) - (flux_n[:height] - flux_y[:height]))
             return carry
 
         lax.fori_loop(0, levels, level, 0, unroll=UNROLL)
-
-    shift = (partner[0] + lon * LANES) & (nlon * LANES - 1)
-    tile, offset = shift // LANES, shift & (LANES - 1)
-    tile_far, tile_place = tile // WIDE, lax.rem(tile, WIDE)
-    edge_lane = lax.broadcasted_iota(jnp.int32, (EDGE, LANES), 1)
-    order = (offset - edge_lane) & (LANES - 1)
-    near_part = edge_lane <= offset
-    borrow0 = jnp.where(tile_place < place, 1, 0)
-    borrow1 = jnp.where(tile_place - 1 < place, 1, 0)
-
-    near_slots = [lax.rem(2 * place - tile_place + i + WIDE, WIDE) for i in range(2)]
-    far_slots = [lax.rem(2 * far - tile_far + borrow + 2 * groups, groups) for borrow in (borrow0, borrow1)]
 
     def wait_hop(step, tracer, near):
         for k in peers(near):
@@ -294,28 +323,17 @@
         for tracer, near in ((0, False), (1, True)):
             wait_hop(step, tracer, near)
             first, second = picked(step, tracer, near)
-            over[tracer] = jnp.where(near_part, first, second)
-
-    for copy in first_rows[:6]:
+            over[step, tracer] = jnp.where(near_part, first, second)
+
+    for copy in first_rows:
         copy.wait()
     north[0, 1, pl.ds(2 * levels, levels)] = land_rows[0].astype(F32)
-    pl.semaphore_wait(barrier, expected)
+    south[0, 1, pl.ds(2 * levels, levels)] = land_rows[1].astype(F32)
 
     @pl.when(top)
     def _():
+        pl.semaphore_wait(barrier, expected)
         first_hop(0)
-
-    @pl.when(lat < nlat - 1)
-    def _():
-        to_north(0).start()
-
-    for copy in first_rows[6:]:
-        copy.wait()
-    south[0, 1, pl.ds(2 * levels, levels)] = land_rows[1].astype(F32)
-
-    @pl.when(lat > 0)
-    def _():
-        to_south(0).start()
 
     for load in loads:
         load.wait()
@@ -325,11 +343,42 @@
         return carry
 
     lax.fori_loop(0, levels, ocean, 0, unroll=UNROLL)
+    pack_cols(0)
+    lay_kappas()
+
+    @pl.when(top)
+    def _():
+        crown()
+
+    @pl.when(jnp.logical_not(top))
+    def _():
+        pl.semaphore_wait(barrier, expected)
+
+    @pl.when(lat < nlat - 1)
+    def _():
+        to_north(0).start()
+
+    @pl.when(lat > 0)
+    def _():
+        to_south(0).start()
+
+    shift = (partner[0] + lon * LANES) & (nlon * LANES - 1)
+    tile, offset = shift // LANES, shift & (LANES - 1)
+    tile_far, tile_place = tile // WIDE, lax.rem(tile, WIDE)
+    edge_lane = lax.broadcasted_iota(jnp.int32, (EDGE, LANES), 1)
+    order = (offset - edge_lane) & (LANES - 1)
+    near_part = edge_lane <= offset
+    borrow0 = jnp.where(tile_place < place, 1, 0)
+    borrow1 = jnp.where(tile_place - 1 < place, 1, 0)
+
+    near_slots = [lax.rem(2 * place - tile_place + i + WIDE, WIDE) for i in range(2)]
+    far_slots = [lax.rem(2 * far - tile_far + borrow + 2 * groups, groups) for borrow in (borrow0, borrow1)]
 
     for step in range(STEPS):
         last = step == STEPS - 1
         t_out, s_out, at = (temp_out, salt_out, 0) if last else (t_ext.at[step + 1], s_ext.at[step + 1], HALO)
-        pack_cols(step)
+        if step:
+            pack_cols(step)
         to_right(step).start()
         to_left(step).start()
 
@@ -346,12 +395,12 @@
         @pl.when(lat < nlat - 1)
         def _():
             to_south(step).wait_recv()
-            lay_north(step, above.at[step], False)
+            lay(step, above.at[step], end, end)
 
         to_right(step).wait_recv()
         to_left(step).wait_recv()
         make_faces(step)
-        advance(step, 0, height, t_out, s_out, at)
+        advance(step, t_out, s_out, at)
         if not last:
             pack_rows(step + 1, south, HALO)
 
@@ -359,22 +408,22 @@
             def _():
                 to_south(step + 1).start()
 
-        @pl.when(top)
-        def _():
-            choose(step)
-            lay_north(step, over, True)
-            advance(step, height - 8, 8, t_out, s_out, at)
-
-        if not last:
             pack_rows(step + 1, north, end - 2)
-
-            @pl.when(top)
-            def _():
-                first_hop(step + 1)
 
             @pl.when(lat < nlat - 1)
             def _():
                 to_north(step + 1).start()
+
+        @pl.when(top)
+        def _():
+            choose(step)
+            mend(step)
+            if not last:
+                both = pl.ds(0, 2 * levels)
+                for tracer in range(2):
+                    north[step + 1, tracer, both] = north[step + 1, tracer, both] - mending[tracer, both]
+                first_hop(step + 1)
+            mend_rows(t_out, s_out, at + height - 2)
 
     for step in range(STEPS):
         to_right(step).wait_send()
@@ -396,23 +445,30 @@
                         hop(step, tracer, near, k).wait_send()
 
 
+def hand_over(temp, salt, temp_out, salt_out):
+    temp_out[...] = temp[...]
+    salt_out[...] = salt[...]
+
+
 def local(nlon, nlat, temp, salt, u_vel, v_vel, land_sea, partner, kappa_h, kappa_v):
     levels, height, width = temp.shape
     block = jax.ShapeDtypeStruct(temp.shape, F32)
     anywhere = pl.BlockSpec(memory_space=pl.ANY)
-    numbers = pl.BlockSpec(memory_space=pltpu.SMEM)
     groups = nlon // WIDE
 
     def room(*shape):
         return pltpu.VMEM(shape, F32)
 
     tall = height + 24
-    return pl.pallas_call(
+    results = pl.pallas_call(
         functools.partial(kernel, nlon, nlat),
         out_shape=(block, block),
-        in_specs=[anywhere] * 5 + [numbers] * 3,
+        in_specs=[anywhere] * 8,
         out_specs=[pl.BlockSpec(memory_space=pltpu.VMEM)] * 2,
         scratch_shapes=[
+            pltpu.SMEM(partner.shape, jnp.int32),
+            pltpu.SMEM(kappa_h.shape, F32),
+            pltpu.SMEM(kappa_v.shape, F32),
             room(STEPS, levels, tall, width),
             room(STEPS, levels, tall, width),
             room(levels, tall, width),
@@ -431,10 +487,13 @@
             *[room(WIDE, EDGE, width)] * (2 * STEPS),
             *[room(groups, EDGE, width)] * (2 * STEPS),
             room(2, EDGE, width),
+            room(STEPS, 2, EDGE, width),
+            room(3, 16, width),
             room(2, EDGE, width),
             room(height, width),
             room(height, width),
-            pltpu.SemaphoreType.DMA((5,)),
+            room(height, width),
+            pltpu.SemaphoreType.DMA((8,)),
             pltpu.SemaphoreType.DMA((12,)),
             pltpu.SemaphoreType.DMA((STEPS, 4)),
             pltpu.SemaphoreType.DMA((STEPS, 4)),
@@ -446,6 +505,15 @@
         compiler_params=pltpu.CompilerParams(collective_id=0, has_side_effects=True, vmem_limit_bytes=60 << 20),
         name="tracer_steps",
     )(temp, salt, u_vel, v_vel, land_sea, partner, kappa_h, kappa_v)
+    return pl.pallas_call(
+        hand_over,
+        out_shape=(block, block),
+        grid=(2,),
+        in_specs=[pl.BlockSpec((levels // 2, height, width), lambda i: (i, 0, 0))] * 2,
+        out_specs=[pl.BlockSpec((levels // 2, height, width), lambda i: (i, 0, 0))] * 2,
+        compiler_params=pltpu.CompilerParams(vmem_limit_bytes=60 << 20),
+        name="hand_over",
+    )(*results)
 
 
 def solution(mesh):

time: 33.2 us -> 30.9 us (0.931)
  local copies, waits for them, and re-layouts: 2.3 us -> 0 us
    unnamed x4 -> x0, local copies, waits for them, and re-layouts: 2.3 us -> none
    pallas_call x0 -> x1, Pallas kernels: none -> 1.7 us  [local(): pl.pallas_call(hand_over, out_shape=(block, block), grid=(2,), in_specs=[...]
    pallas_call x1, Pallas kernels: 30.1 us -> 28.5 us  [local(): pl.pallas_call(functools.partial(kernel, nlon, nlat), out_shape=(block, b...]
where the time goes in v4:
time: 30.9 us; the launch traced here: 30.8 us
  Pallas kernels  30.2 us (98%)
  between operations  0.64 us (2%)
    pallas_call x1, Pallas kernels, local(): pl.pallas_call(functools.partial(kernel, nlon, nlat), out_shape=(block, b...  28.5 us
    pallas_call x1, Pallas kernels, local(): pl.pallas_call(hand_over, out_shape=(block, block), grid=(2,), in_specs=[...  1.7 us

profile of v4, /device:TPU:9, one launch (start us, length us, event | category | flops | bytes accessed | tf_op | source)
XLA Modules:
  0.0 30.8 jit_solution(3417747642677608269)
XLA Ops:
  0.6 28.5 %tracer_steps.1 = (f32[10,32,128]{2,1,0:T(8,128)}, f32[10,32,128]{2,1,0:T(8,128)}) custom-call(f32[10,32,128]{2,1,0:T(8,128)} %temp.1, f32[10,32,128]{2,1,0:T(8,128)} %salt.1, f32[10,32,128]{2,1,0:T(8,128)} %u_vel.1, f32[10,32,128]{2,1,0:T(8,128)} %v_vel.1, s32[10,32,128]{2,1,0:T(8,128)} %land.1, s32[128]{0:T(128)} %partner_in.1, f32[10]{0:T(128)} %kappa_h_in.1, ...), custom_call_target="tpu_custom_call" | custom-call | tf_op jit(solution)/shard_map/tracer_steps/pallas_call | solution.py:463
  29.1 1.7 %hand_over.1 = (f32[10,32,128]{2,1,0:T(8,128)}, f32[10,32,128]{2,1,0:T(8,128)}) custom-call(f32[10,32,128]{2,1,0:T(8,128)} %get-tuple-element.4.temp, f32[10,32,128]{2,1,0:T(8,128)} %get-tuple-element.5.salt), custom_call_target="tpu_custom_call" | custom-call | tf_op jit(solution)/shard_map/hand_over/pallas_call | solution.py:508

commit v5 on v4

--- a/solution.py
+++ b/solution.py
@@ -27,8 +27,8 @@
 
 
 def kernel(
-    nlon, nlat, temp, salt, u_vel, v_vel, land, partner_in, kappa_h_in, kappa_v_in, temp_out, salt_out,
-    partner, kappa_h, kappa_v,
+    nlon, nlat, temp, salt, u_vel, v_vel, land, partner_in, kappas_in, temp_out, salt_out,
+    partner, coefficients,
     t_ext, s_ext, v_ext, o_ext, u_own, land_own, land_rows, cols, north, south, relay, west, east, below, above,
     near00, near01, near10, near11, far00, far01, far10, far11, under, over, under_top, mending,
     face_t, face_s, kappas,
@@ -79,11 +79,13 @@
                 (land, land_own),
                 (u_vel, u_own),
                 (partner_in, partner),
-                (kappa_h_in, kappa_h),
-                (kappa_v_in, kappa_v),
+                (kappas_in, coefficients),
             )
         )
     ]
+    for copy in first_rows[:6]:
+        copy.start()
+
     barrier = pltpu.get_barrier_semaphore()
 
     def greet(a, b):
@@ -109,7 +111,7 @@
 
     expected = 2 + jnp.where(lat > 0, 1, 0) + jnp.where(top, WIDE + groups - 2, 1)
 
-    for copy in first_rows + loads:
+    for copy in first_rows[6:] + loads:
         copy.start()
 
     def remote(src, dst, sent, got, a, b):
@@ -206,7 +208,7 @@
             o_ext[l, pl.ds(end, 2)] = above_own
             under_top[0, pl.ds(l, 1)] = v_ext[l, pl.ds(end - 2, 1)]
             under_top[1, pl.ds(l, 1)] = o_ext[l, pl.ds(end - 2, 1)]
-            under_top[2, pl.ds(l, 1)] = jnp.full((1, LANES), kappa_h[l], F32)
+            under_top[2, pl.ds(l, 1)] = jnp.full((1, LANES), coefficients[l], F32)
             return carry
 
         lax.fori_loop(0, levels, level, 0, unroll=UNROLL)
@@ -245,7 +247,7 @@
         kappas[...] = lax.fori_loop(
             0,
             levels,
-            lambda l, k: jnp.where((lane >= l * SLOT) & (lane < (l + 1) * SLOT), kappa_h[l], k),
+            lambda l, k: jnp.where((lane >= l * SLOT) & (lane < (l + 1) * SLOT), coefficients[l], k),
             jnp.zeros((height, LANES), F32),
             unroll=UNROLL,
         )
@@ -270,10 +272,10 @@
 
         def level(l, carry):
             base = l * SLOT
-            diffuse = kappa_h[l]
+            diffuse = coefficients[l]
             down, up = jnp.maximum(l - 1, 0), jnp.minimum(l + 1, levels - 1)
-            k_down = jnp.where(l > 0, kappa_v[down], 0.0)
-            k_up = jnp.where(l < levels - 1, kappa_v[jnp.minimum(l, levels - 2)], 0.0)
+            k_down = jnp.where(l > 0, coefficients[levels + down], 0.0)
+            k_up = jnp.where(l < levels - 1, coefficients[levels + jnp.minimum(l, levels - 2)], 0.0)
             u, o = u_own[l], o_ext[l, here]
             u_next = jnp.where(lane == LANES - 1, roll(other, 118 - base), roll(u, LANES - 1))
             o_next = jnp.where(lane == LANES - 1, roll(other, 116 - base), roll(o, LANES - 1))
@@ -325,16 +327,18 @@
             first, second = picked(step, tracer, near)
             over[step, tracer] = jnp.where(near_part, first, second)
 
-    for copy in first_rows:
+    for copy in first_rows[:6]:
         copy.wait()
     north[0, 1, pl.ds(2 * levels, levels)] = land_rows[0].astype(F32)
-    south[0, 1, pl.ds(2 * levels, levels)] = land_rows[1].astype(F32)
 
     @pl.when(top)
     def _():
         pl.semaphore_wait(barrier, expected)
         first_hop(0)
 
+    for copy in first_rows[6:]:
+        copy.wait()
+    south[0, 1, pl.ds(2 * levels, levels)] = land_rows[1].astype(F32)
     for load in loads:
         load.wait()
 
@@ -445,9 +449,12 @@
                         hop(step, tracer, near, k).wait_send()
 
 
-def hand_over(temp, salt, temp_out, salt_out):
-    temp_out[...] = temp[...]
-    salt_out[...] = salt[...]
+def hand_over(temp, salt, temp_out, salt_out, sem):
+    copies = [pltpu.make_async_copy(a, b, sem.at[i]) for i, (a, b) in enumerate(((temp, temp_out), (salt, salt_out)))]
+    for copy in copies:
+        copy.start()
+    for copy in copies:
+        copy.wait()
 
 
 def local(nlon, nlat, temp, salt, u_vel, v_vel, land_sea, partner, kappa_h, kappa_v):
@@ -463,12 +470,11 @@
     results = pl.pallas_call(
         functools.partial(kernel, nlon, nlat),
         out_shape=(block, block),
-        in_specs=[anywhere] * 8,
+        in_specs=[anywhere] * 7,
         out_specs=[pl.BlockSpec(memory_space=pltpu.VMEM)] * 2,
         scratch_shapes=[
             pltpu.SMEM(partner.shape, jnp.int32),
-            pltpu.SMEM(kappa_h.shape, F32),
-            pltpu.SMEM(kappa_v.shape, F32),
+            pltpu.SMEM((2 * levels - 1,), F32),
             room(STEPS, levels, tall, width),
             room(STEPS, levels, tall, width),
             room(levels, tall, width),
@@ -493,7 +499,7 @@
             room(height, width),
             room(height, width),
             room(height, width),
-            pltpu.SemaphoreType.DMA((8,)),
+            pltpu.SemaphoreType.DMA((7,)),
             pltpu.SemaphoreType.DMA((12,)),
             pltpu.SemaphoreType.DMA((STEPS, 4)),
             pltpu.SemaphoreType.DMA((STEPS, 4)),
@@ -502,18 +508,10 @@
             pltpu.SemaphoreType.DMA((STEPS, 2, groups)),
             pltpu.SemaphoreType.DMA((STEPS, 2, groups)),
         ],
-        compiler_params=pltpu.CompilerParams(collective_id=0, has_side_effects=True, vmem_limit_bytes=60 << 20),
+        compiler_params=pltpu.CompilerParams(collective_id=0, has_side_effects=True, vmem_limit_bytes=54880 << 10),
         name="tracer_steps",
-    )(temp, salt, u_vel, v_vel, land_sea, partner, kappa_h, kappa_v)
-    return pl.pallas_call(
-        hand_over,
-        out_shape=(block, block),
-        grid=(2,),
-        in_specs=[pl.BlockSpec((levels // 2, height, width), lambda i: (i, 0, 0))] * 2,
-        out_specs=[pl.BlockSpec((levels // 2, height, width), lambda i: (i, 0, 0))] * 2,
-        compiler_params=pltpu.CompilerParams(vmem_limit_bytes=60 << 20),
-        name="hand_over",
-    )(*results)
+    )(temp, salt, u_vel, v_vel, land_sea, partner, jnp.concatenate([kappa_h, kappa_v]))
+    return results
 
 
 def solution(mesh):

time: 30.9 us -> 30.5 us (0.987)
  Pallas kernels: 30.2 us -> 27.7 us
  local copies, waits for them, and re-layouts: 0 us -> 1.34 us
  other arithmetic: 0 us -> 0.75 us
    pallas_call x1 -> x0, Pallas kernels: 1.7 us -> none  [local(): pl.pallas_call(hand_over, out_shape=(block, block), grid=(2,), in_specs=[...]
    unnamed x0 -> x4, local copies, waits for them, and re-layouts: none -> 1.34 us
    pallas_call x1, Pallas kernels: 28.5 us -> 27.7 us  [local(): pl.pallas_call(functools.partial(kernel, nlon, nlat), out_shape=(block, b...]
    concatenate x0 -> x1, other arithmetic: none -> 0.75 us  [local(): jnp.concatenate([kappa_h, kappa_v])]
where the time goes in v5:
time: 30.5 us; the launch traced here: 30.4 us
  Pallas kernels  27.7 us (91%)
  local copies, waits for them, and re-layouts  1.34 us (4%)
  other arithmetic  0.75 us (2%)
  between operations  0.65 us (2%)
    pallas_call x1, Pallas kernels, local(): pl.pallas_call(functools.partial(kernel, nlon, nlat), out_shape=(block, b...  27.7 us
    unnamed x4, local copies, waits for them, and re-layouts  1.34 us
    concatenate x1, other arithmetic, local(): jnp.concatenate([kappa_h, kappa_v])  0.75 us

profile of v5, /device:TPU:9, one launch (start us, length us, event | category | flops | bytes accessed | tf_op | source)
XLA Modules:
  0.0 30.4 jit_solution(14458229642852905435)
XLA Ops:
  0.6 0.0 copy-start
  0.6 0.8 %pad_maximum_fusion.kappas_in = f32[19]{0:T(128)S(1)} fusion(f32[9]{0:T(128)} %param.15, f32[10]{0:T(128)} %param.14), kind=kLoop, calls=%fused_computation | loop fusion | flops 19 | bytes 152 | tf_op jit(solution)/shard_map/concatenate | solution.py:513
  1.4 0.0 copy-done
  1.4 27.7 %tracer_steps.1 = (f32[10,32,128]{2,1,0:T(8,128)S(1)}, f32[10,32,128]{2,1,0:T(8,128)S(1)}) custom-call(f32[10,32,128]{2,1,0:T(8,128)} %temp.1, f32[10,32,128]{2,1,0:T(8,128)} %salt.1, f32[10,32,128]{2,1,0:T(8,128)} %u_vel.1, f32[10,32,128]{2,1,0:T(8,128)} %v_vel.1, s32[10,32,128]{2,1,0:T(8,128)} %land.1, s32[128]{0:T(128)S(1)} %copy-done, ...), custom_call_target="tpu_custom_call" | custom-call | tf_op jit(solution)/shard_map/tracer_steps/pallas_call | solution.py:470
  29.1 0.7 %copy.12 = f32[10,32,128]{2,1,0:T(8,128)} copy(f32[10,32,128]{2,1,0:T(8,128)S(1)} %get-tuple-element.4) | data formatting | bytes 327680
  29.8 0.7 %copy.13 = f32[10,32,128]{2,1,0:T(8,128)} copy(f32[10,32,128]{2,1,0:T(8,128)S(1)} %get-tuple-element.5) | data formatting | bytes 327680
Async XLA Ops:
  0.6 0.8 %copy-start = (s32[128]{0:T(128)S(1)}, s32[128]{0:T(128)}, u32[]{:S(2)}) copy-start(s32[128]{0:T(128)} %partner_in.1) | copy-start | bytes 1540

commit v6 on v5

--- a/solution.py
+++ b/solution.py
@@ -83,9 +83,6 @@
             )
         )
     ]
-    for copy in first_rows[:6]:
-        copy.start()
-
     barrier = pltpu.get_barrier_semaphore()
 
     def greet(a, b):
@@ -93,10 +90,10 @@
 
     @pl.when(top)
     def _():
-        for k in range(1, WIDE):
+        for k in farthest_first(groups):
+            greet(in_across(k), lat)
+        for k in farthest_first(WIDE):
             greet(in_group(k), lat)
-        for k in range(1, groups):
-            greet(in_across(k), lat)
 
     greet(right, lat)
     greet(left, lat)
@@ -111,7 +108,7 @@
 
     expected = 2 + jnp.where(lat > 0, 1, 0) + jnp.where(top, WIDE + groups - 2, 1)
 
-    for copy in first_rows[6:] + loads:
+    for copy in first_rows + loads:
         copy.start()
 
     def remote(src, dst, sent, got, a, b):
@@ -262,42 +259,55 @@
             opened = at(theirs, 10 - back) * at(mine, 11 - back)
             ref[...] = flux(at(theirs, 1), at(mine, 2), theirs, at(mine, 3), speed, opened, kappas[...])
 
-    def advance(step, t_out, s_out, shift):
-        here, tall = own, height + 8
-        theirs, other = west[step], east[step]
-        faces = (face_t[...], face_s[...])
+    def advance_yz(step, t_out, s_out, shift):
+        tall = height + 8
 
         def rise(k):
             return pl.ds(HALO - 1 + k, tall)
 
         def level(l, carry):
-            base = l * SLOT
             diffuse = coefficients[l]
             down, up = jnp.maximum(l - 1, 0), jnp.minimum(l + 1, levels - 1)
             k_down = jnp.where(l > 0, coefficients[levels + down], 0.0)
             k_up = jnp.where(l < levels - 1, coefficients[levels + jnp.minimum(l, levels - 2)], 0.0)
-            u, o = u_own[l], o_ext[l, here]
+            o = o_ext[l, own]
+            speed_y = v_ext[l, rise(0)] + v_ext[l, rise(1)]
+            open_y = o_ext[l, rise(0)] * o_ext[l, rise(1)]
+            lift = k_up * (o * o_ext[up, own])
+            drop = k_down * (o * o_ext[down, own])
+            for ext, out in ((t_ext, t_out), (s_ext, s_out)):
+                c = ext[step, l, own]
+                flux_y = flux(
+                    ext[step, l, rise(0)], ext[step, l, rise(1)], ext[step, l, rise(-1)], ext[step, l, rise(2)],
+                    speed_y, open_y, diffuse,
+                )
+                flux_n = roll(flux_y, tall - 1, 0)
+                gain = lift * (ext[step, up, own] - c) - drop * (c - ext[step, down, own])
+                out[l, pl.ds(shift, height)] = c + o * (gain - (flux_n[:height] - flux_y[:height]))
+            return carry
+
+        lax.fori_loop(0, levels, level, 0, unroll=UNROLL)
+
+    def advance_x(step, t_out, s_out, shift):
+        theirs, other = west[step], east[step]
+        faces = (face_t[...], face_s[...])
+
+        def level(l, carry):
+            base = l * SLOT
+            diffuse = coefficients[l]
+            u, o = u_own[l], o_ext[l, own]
             u_next = jnp.where(lane == LANES - 1, roll(other, 118 - base), roll(u, LANES - 1))
             o_next = jnp.where(lane == LANES - 1, roll(other, 116 - base), roll(o, LANES - 1))
             speed_x, open_x = u + u_next, o * o_next
-            speed_y = v_ext[l, rise(0)] + v_ext[l, rise(1)]
-            open_y = o_ext[l, rise(0)] * o_ext[l, rise(1)]
-            lift = k_up * (o * o_ext[up, here])
-            drop = k_down * (o * o_ext[down, here])
             for ext, out, face, back in ((t_ext, t_out, faces[0], 0), (s_ext, s_out, faces[1], 4)):
-                c = ext[step, l, here]
+                c = ext[step, l, own]
                 before = jnp.where(lane == 0, roll(theirs, 127 - back - base), roll(c, 1))
                 next1 = jnp.where(lane == LANES - 1, roll(other, 125 - back - base), roll(c, LANES - 1))
                 next2 = jnp.where(lane >= LANES - 2, roll(other, 124 - back - base), roll(c, LANES - 2))
                 flux_x = flux(c, next1, before, next2, speed_x, open_x, diffuse)
                 flux_w = jnp.where(lane == 0, roll(face, lax.rem(2 * LANES - back - base, LANES)), roll(flux_x, 1))
-                flux_y = flux(
-                    ext[step, l, rise(0)], ext[step, l, rise(1)], ext[step, l, rise(-1)], ext[step, l, rise(2)],
-                    speed_y, open_y, diffuse,
-                )
-                flux_n = roll(flux_y, tall - 1, 0)
-                gain = lift * (ext[step, up, here] - c) - drop * (c - ext[step, down, here])
-                out[l, pl.ds(shift, height)] = c + o * (gain - (flux_x - flux_w) - (flux_n[:height] - flux_y[:height]))
+                here = pl.ds(shift, height)
+                out[l, here] = out[l, here] - o * (flux_x - flux_w)
             return carry
 
         lax.fori_loop(0, levels, level, 0, unroll=UNROLL)
@@ -311,7 +321,7 @@
         return slots[step][tracer][at[0]], slots[step][tracer][at[1]]
 
     def second_hop(step):
-        for tracer, near in ((0, True), (1, False)):
+        for tracer, near in ((1, False), (0, True)):
             wait_hop(step, tracer, near)
             first, second = picked(step, tracer, near)
             first = jnp.take_along_axis(first, order, axis=1)
@@ -348,23 +358,32 @@
 
     lax.fori_loop(0, levels, ocean, 0, unroll=UNROLL)
     pack_cols(0)
+
+    @pl.when(jnp.logical_not(top))
+    def _():
+        pl.semaphore_wait(barrier, expected)
+
+    to_right(0).start()
+    to_left(0).start()
+
+    @pl.when(lat < nlat - 1)
+    def _():
+        to_north(0).start()
+
+    @pl.when(lat > 0)
+    def _():
+        to_south(0).start()
+
     lay_kappas()
 
     @pl.when(top)
     def _():
         crown()
 
-    @pl.when(jnp.logical_not(top))
-    def _():
-        pl.semaphore_wait(barrier, expected)
-
-    @pl.when(lat < nlat - 1)
-    def _():
-        to_north(0).start()
-
-    @pl.when(lat > 0)
-    def _():
-        to_south(0).start()
+    def send_cols(step):
+        pack_cols(step)
+        to_right(step).start()
+        to_left(step).start()
 
     shift = (partner[0] + lon * LANES) & (nlon * LANES - 1)
     tile, offset = shift // LANES, shift & (LANES - 1)
@@ -382,9 +401,10 @@
         last = step == STEPS - 1
         t_out, s_out, at = (temp_out, salt_out, 0) if last else (t_ext.at[step + 1], s_ext.at[step + 1], HALO)
         if step:
-            pack_cols(step)
-        to_right(step).start()
-        to_left(step).start()
+
+            @pl.when(top)
+            def _():
+                send_cols(step)
 
         @pl.when(top)
         def _():
@@ -401,11 +421,17 @@
             to_south(step).wait_recv()
             lay(step, above.at[step], end, end)
 
+        advance_yz(step, t_out, s_out, at)
         to_right(step).wait_recv()
         to_left(step).wait_recv()
         make_faces(step)
-        advance(step, t_out, s_out, at)
+        advance_x(step, t_out, s_out, at)
         if not last:
+
+            @pl.when(jnp.logical_not(top))
+            def _():
+                send_cols(step + 1)
+
             pack_rows(step + 1, south, HALO)
 
             @pl.when(lat > 0)

time: 30.5 us -> 30 us (0.984)
  Pallas kernels: 27.7 us -> 27.1 us
    pallas_call x1, Pallas kernels: 27.7 us -> 27.1 us  [local(): pl.pallas_call(functools.partial(kernel, nlon, nlat), out_shape=(block, b...]
where the time goes in v6:
time: 30 us; the launch traced here: 29.9 us
  Pallas kernels  27.1 us (90%)
  local copies, waits for them, and re-layouts  1.34 us (4%)
  other arithmetic  0.75 us (2%)
  between operations  0.65 us (2%)
    pallas_call x1, Pallas kernels, local(): pl.pallas_call(functools.partial(kernel, nlon, nlat), out_shape=(block, b...  27.1 us
    unnamed x4, local copies, waits for them, and re-layouts  1.34 us
    concatenate x1, other arithmetic, local(): jnp.concatenate([kappa_h, kappa_v])  0.75 us

profile of v6, /device:TPU:9, one launch (start us, length us, event | category | flops | bytes accessed | tf_op | source)
XLA Modules:
  0.0 29.9 jit_solution(2272209669304435207)
XLA Ops:
  0.6 0.0 copy-start
  0.6 0.8 %pad_maximum_fusion.kappas_in = f32[19]{0:T(128)S(1)} fusion(f32[9]{0:T(128)} %param.15, f32[10]{0:T(128)} %param.14), kind=kLoop, calls=%fused_computation | loop fusion | flops 19 | bytes 152 | tf_op jit(solution)/shard_map/concatenate | solution.py:539
  1.4 0.0 copy-done
  1.4 27.1 %tracer_steps.1 = (f32[10,32,128]{2,1,0:T(8,128)S(1)}, f32[10,32,128]{2,1,0:T(8,128)S(1)}) custom-call(f32[10,32,128]{2,1,0:T(8,128)} %temp.1, f32[10,32,128]{2,1,0:T(8,128)} %salt.1, f32[10,32,128]{2,1,0:T(8,128)} %u_vel.1, f32[10,32,128]{2,1,0:T(8,128)} %v_vel.1, s32[10,32,128]{2,1,0:T(8,128)} %land.1, s32[128]{0:T(128)S(1)} %copy-done, ...), custom_call_target="tpu_custom_call" | custom-call | tf_op jit(solution)/shard_map/tracer_steps/pallas_call | solution.py:496
  28.5 0.7 %copy.12 = f32[10,32,128]{2,1,0:T(8,128)} copy(f32[10,32,128]{2,1,0:T(8,128)S(1)} %get-tuple-element.4) | data formatting | bytes 327680
  29.2 0.7 %copy.13 = f32[10,32,128]{2,1,0:T(8,128)} copy(f32[10,32,128]{2,1,0:T(8,128)S(1)} %get-tuple-element.5) | data formatting | bytes 327680
Async XLA Ops:
  0.6 0.8 %copy-start = (s32[128]{0:T(128)S(1)}, s32[128]{0:T(128)}, u32[]{:S(2)}) copy-start(s32[128]{0:T(128)} %partner_in.1) | copy-start | bytes 1540

commit v7 on v6

--- a/solution.py
+++ b/solution.py
@@ -27,7 +27,7 @@
 
 
 def kernel(
-    nlon, nlat, temp, salt, u_vel, v_vel, land, partner_in, kappas_in, temp_out, salt_out,
+    nlon, nlat, temp, salt, u_vel, v_vel, land, partner_in, kappas_in, temp_out, salt_out, unit,
     partner, coefficients,
     t_ext, s_ext, v_ext, o_ext, u_own, land_own, land_rows, cols, north, south, relay, west, east, below, above,
     near00, near01, near10, near11, far00, far01, far10, far11, under, over, under_top, mending,
@@ -375,6 +375,7 @@
         to_south(0).start()
 
     lay_kappas()
+    unit[...] = jnp.ones_like(unit)
 
     @pl.when(top)
     def _():
@@ -493,11 +494,11 @@
         return pltpu.VMEM(shape, F32)
 
     tall = height + 24
-    results = pl.pallas_call(
+    new_temp, new_salt, unit = pl.pallas_call(
         functools.partial(kernel, nlon, nlat),
-        out_shape=(block, block),
+        out_shape=(block, block, jax.ShapeDtypeStruct((width,), F32)),
         in_specs=[anywhere] * 7,
-        out_specs=[pl.BlockSpec(memory_space=pltpu.VMEM)] * 2,
+        out_specs=[pl.BlockSpec(memory_space=pltpu.VMEM)] * 3,
         scratch_shapes=[
             pltpu.SMEM(partner.shape, jnp.int32),
             pltpu.SMEM((2 * levels - 1,), F32),
@@ -537,7 +538,7 @@
         compiler_params=pltpu.CompilerParams(collective_id=0, has_side_effects=True, vmem_limit_bytes=54880 << 10),
         name="tracer_steps",
     )(temp, salt, u_vel, v_vel, land_sea, partner, jnp.concatenate([kappa_h, kappa_v]))
-    return results
+    return new_temp * unit, new_salt * unit
 
 
 def solution(mesh):

time: 30 us -> 29.4 us (0.980)
  local copies, waits for them, and re-layouts: 1.34 us -> 0.01 us
  other arithmetic: 0.75 us -> 1.5 us
    unnamed x4 -> x2, local copies, waits for them, and re-layouts: 1.34 us -> 0.01 us
    mul x0 -> x1, other arithmetic: none -> 0.75 us  [local(): return (new_temp * unit, new_salt * unit)]
where the time goes in v7:
time: 29.4 us; the launch traced here: 29.3 us
  Pallas kernels  27.1 us (92%)
  other arithmetic  1.5 us (5%)
  between operations  0.65 us (2%)
    pallas_call x1, Pallas kernels, local(): pl.pallas_call(functools.partial(kernel, nlon, nlat), out_shape=(block, b...  27.1 us
    concatenate x1, other arithmetic, local(): jnp.concatenate([kappa_h, kappa_v])  0.75 us
    mul x1, other arithmetic, local(): return (new_temp * unit, new_salt * unit)  0.75 us

profile of v7, /device:TPU:9, one launch (start us, length us, event | category | flops | bytes accessed | tf_op | source)
XLA Modules:
  0.0 29.3 jit_solution(14316812036904857666)
XLA Ops:
  0.6 0.0 copy-start
  0.6 0.8 %pad_maximum_fusion.kappas_in = f32[19]{0:T(128)S(1)} fusion(f32[9]{0:T(128)} %param.15, f32[10]{0:T(128)} %param.14), kind=kLoop, calls=%fused_computation.2 | loop fusion | flops 19 | bytes 152 | tf_op jit(solution)/shard_map/concatenate | solution.py:540
  1.4 0.0 copy-done
  1.4 27.1 %tracer_steps.1 = (f32[10,32,128]{2,1,0:T(8,128)S(1)}, f32[10,32,128]{2,1,0:T(8,128)S(1)}, f32[128]{0:T(128)S(1)}) custom-call(f32[10,32,128]{2,1,0:T(8,128)} %temp.1, f32[10,32,128]{2,1,0:T(8,128)} %salt.1, f32[10,32,128]{2,1,0:T(8,128)} %u_vel.1, f32[10,32,128]{2,1,0:T(8,128)} %v_vel.1, s32[10,32,128]{2,1,0:T(8,128)} %land.1, s32[128]{0:T(128)S(1)} %copy-done, ...), custom_call_target="tpu_custom_call" | custom-call | tf_op jit(solution)/shard_map/tracer_steps/pallas_call | solution.py:497
  28.5 0.8 %broadcast_multiply_fusion = (f32[10,32,128]{2,1,0:T(8,128)}, f32[10,32,128]{2,1,0:T(8,128)}) fusion(f32[10,32,128]{2,1,0:T(8,128)S(1)} %get-tuple-element.7, f32[128]{0:T(128)S(1)} %get-tuple-element.6, f32[10,32,128]{2,1,0:T(8,128)S(1)} %get-tuple-element.5), kind=kLoop, calls=%fused_computation | loop fusion | flops 81920 | bytes 655872 | tf_op jit(solution)/shard_map/mul | solution.py:541
Async XLA Ops:
  0.6 0.8 %copy-start = (s32[128]{0:T(128)S(1)}, s32[128]{0:T(128)}, u32[]{:S(2)}) copy-start(s32[128]{0:T(128)} %partner_in.1) | copy-start | bytes 1540
